TPU v7x, 32 devices: a whole 2x2x4 slice. The times are simulated.
32 devices in a mesh: section: 2 (over core), dp: 16 (over z, y, x).
Axes of the slice: x: 2, y: 2, z: 4, core: 2. Of those that a mesh axis runs over, the one named last changes fastest.
Arguments:
- source: bfloat16 [2, 4096, 1024], P(None, 'dp'), may hold values from -6 to 6
- target: bfloat16 [2, 2048, 1024], P(None, 'dp'), may hold values from -6 to 6
- cotangent: bfloat16 [2, 2048, 1024], P(None, 'dp'), may hold values from -6 to 6
- source_lengths: int32 [2, 16], P(None, 'dp'), may hold values from 64 to 256, as said below
- target_lengths: int32 [2, 16], P(None, 'dp'), may hold values from 64 to 128, as said below
- attention_in: bfloat16 [2, 1024, 3072], P('section'), may hold values from -0.1875 to 0.1875
- attention_out: bfloat16 [2, 1024, 1024], P('section'), may hold values from -2 to 2
- cross_query: bfloat16 [1024, 1024], replicated, may hold values from -0.1875 to 0.1875
- cross_pair: bfloat16 [1024, 2048], replicated, may hold values from -0.1875 to 0.1875
- cross_output: bfloat16 [1024, 1024], replicated, may hold values from -2 to 2
- feed_in: bfloat16 [2, 1024, 4096], P('section'), may hold values from -0.1875 to 0.1875
- feed_out: bfloat16 [2, 4096, 1024], P('section'), may hold values from -0.09375 to 0.09375
- adapter_in: bfloat16 [2, 1024, 512], P('section'), may hold values from -0.1875 to 0.1875
- adapter_in_bias: bfloat16 [2, 512], P('section'), may hold values from -3 to 3
- adapter_out: bfloat16 [2, 512, 1024], P('section'), may hold values from -0.0625 to 0.0625
- adapter_out_bias: bfloat16 [2, 1024], P('section'), may hold values from -1.1953125 to 1.1953125
- prefix: bfloat16 [2, 2, 30, 1024], P('section'), may hold values from -6 to 6
- norm_gains: bfloat16 [2, 3, 1024], P('section'), may hold values from 0.099609375 to 1.8984375
Outputs:
- token_results: bfloat16 [2, 2, 4096, 1024], P('section', None, 'dp')
- prefix_grad: float32 [2, 2, 30, 1024], P('section')
- adapter_in_grad: float32 [2, 1024, 512], P('section', 'dp')
- adapter_out_grad: float32 [2, 512, 1024], P('section', 'dp')
- adapter_in_bias_grad: float32 [2, 512], P('section')
- adapter_out_bias_grad: float32 [2, 1024], P('section')
Inputs may be any that keep to these rules, and one draw needn't show every extreme that they name: `source_lengths`: in every micro-batch at least one pair's source fills all 256 rows. `target_lengths`: in every micro-batch at least one pair's target fills all 128 rows.
All inputs are finite; a program needn't handle non-finite values.
Results may differ from a plain program's by a relative error of at most 0.019.
Values may be sent and summed in bfloat16 or wider, within the bound.
A program may use at most 192 MiB of HBM per device.

v0:
```python
import math

import jax
import jax.numpy as jnp
from jax import lax
from jax.experimental import pallas as pl
from jax.experimental.pallas import tpu as pltpu
from jax.sharding import PartitionSpec as P

BF = jnp.bfloat16
F32 = jnp.float32
MESH = pl.DeviceIdType.MESH
EPS = 1e-05
NEG = -1e30
ROOT_HALF = 0.7071067811865476
INV_ROOT_TWO_PI = 0.3989422804014327
PRE = 30
PRE_PAD = 32
PAIR = 128
HALF = 64
LN_ROWS = 64


def dot(a, b):
    return jnp.dot(a, b, preferred_element_type=F32)


def dot_t(a, b):
    return lax.dot_general(a, b, (((1,), (1,)), ((), ())), preferred_element_type=F32)


def tdot(a, b):
    return lax.dot_general(a, b, (((0,), (0,)), ((), ())), preferred_element_type=F32)


def gelu_and_slope(v):
    cdf = 0.5 + 0.5 * lax.erf(v * ROOT_HALF)
    return v * cdf, cdf + v * (jnp.exp(-0.5 * v * v) * INV_ROOT_TWO_PI)


def rows_of(start, count):
    return pl.ds(pl.multiple_of(start, count), count)


def by_rows(count, body):
    def step(i, carry):
        body(rows_of(i * LN_ROWS, LN_ROWS))
        return carry

    lax.fori_loop(0, count // LN_ROWS, step, 0)


def norm_of(total):
    centre = total - jnp.mean(total, axis=-1, keepdims=True)
    factor = lax.rsqrt(jnp.mean(centre * centre, axis=-1, keepdims=True) + EPS)
    return centre * factor, factor


def norm_back(grad, shaped, factor, gain):
    scaled = grad * gain
    centred = scaled - jnp.mean(scaled, axis=-1, keepdims=True)
    return factor * (centred - shaped * jnp.mean(scaled * shaped, axis=-1, keepdims=True))


def both_heads(block):
    first = lax.broadcasted_iota(jnp.int32, block.shape, 1) < HALF
    zero = jnp.zeros_like(block)
    return jnp.concatenate([jnp.where(first, block, zero), jnp.where(first, zero, block)], axis=0)


def attend(rows, tokens, prefixed, pairs, q, k, vt, vtp, probs, bias, out_t):
    def step(p, carry):
        lanes = rows_of(p * PAIR, PAIR)
        scores = dot_t(k[:, lanes], both_heads(q[:, lanes]))
        shift = bias[...]
        scores = scores + jnp.concatenate([shift] * (2 * rows // PAIR), axis=1)
        power = jnp.exp(scores - jnp.max(scores, axis=0, keepdims=True))
        low = (power * (1.0 / jnp.sum(power, axis=0, keepdims=True))).astype(BF)
        probs(p)[...] = low
        for a in range(2):
            head = rows_of(p * PAIR + a * HALF, HALF)
            part = low[:, a * rows : (a + 1) * rows]
            mixed = dot(vt[head, :], part[:tokens])
            if prefixed:
                mixed = mixed + dot(vtp[head, :], part[tokens:])
            out_t[head, :] = mixed.astype(BF)
        return carry

    lax.fori_loop(0, pairs, step, 0, unroll=4)


def attend_back(rows, tokens, prefixed, pairs, grad, q, k, v, kt, ktp, probs, dq_t, dk, dv, pre_sum):
    def step(p, carry):
        lanes = rows_of(p * PAIR, PAIR)
        grads = both_heads(grad[:, lanes])
        queries = both_heads(q[:, lanes])
        low = probs(p)[...]
        wide = low.astype(F32)
        grad_probs = dot_t(v[:, lanes], grads)
        inner = jnp.sum(wide * grad_probs, axis=0, keepdims=True)
        grad_scores = (wide * (grad_probs - inner)).astype(BF)
        grad_keys = dot(grad_scores, queries)
        grad_values = dot(low, grads)
        dk[:, lanes] = grad_keys[:tokens].astype(BF)
        dv[:, lanes] = grad_values[:tokens].astype(BF)
        if prefixed:
            pre_sum[0, :, lanes] = pre_sum[0, :, lanes] + grad_keys[tokens:]
            pre_sum[1, :, lanes] = pre_sum[1, :, lanes] + grad_values[tokens:]
        for a in range(2):
            head = rows_of(p * PAIR + a * HALF, HALF)
            part = grad_scores[:, a * rows : (a + 1) * rows]
            back = dot(kt[head, :], part[:tokens])
            if prefixed:
                back = back + dot(ktp[head, :], part[tokens:])
            dq_t[head, :] = (back * 0.125).astype(BF)
        return carry

    lax.fori_loop(0, pairs, step, 0, unroll=4)


def make_kernel(nz, ny, nx, features, hidden, adapt, src_rows, tgt_rows):
    chunks = hidden // features
    pairs = features // PAIR
    dp = nz * ny * nx
    ra = features // dp
    enc_keys = src_rows + PRE_PAD
    dec_keys = tgt_rows + PRE_PAD
    small_rows = 2 * PRE_PAD

    def kernel(
        src, tgt, ct, sl, tl, ai, ao, cq, cp, co, fi, fo, di, do, bi, bo, prefix, gains,
        tok, ig_out, og_out, sm_out,
        w, wdi, wdo, pw, k, v, kt, tt, ot, ktp, vtp, xh1, xh2, r1, r2, sa, rb, dz, snd, rcv,
        f1, dqkv, rsx, rsy, rsz, rsa, rsb, rsc, pre_sum, bias, ib_sum, ob_sum,
        small, small_in, small_mid, small_z, small_end, small_all,
        dxin, dct, da, kc, vc, kct,
        wsem, xsem, osem, ssem, rsem, gss, grs, mss, mrs,
    ):
        section = lax.axis_index("section")
        here = lax.axis_index("dp")
        at = {"x": lax.rem(here, nx), "y": lax.rem(here // nx, ny), "z": here // (nx * ny)}
        size = {"x": nx, "y": ny, "z": nz}

        def peer(axis, step):
            c = dict(at)
            c[axis] = lax.rem(at[axis] + step, size[axis])
            return c[axis], (section, (c["z"] * ny + c["y"]) * nx + c["x"])

        other = (1 - section, here)
        barrier = pltpu.get_barrier_semaphore()
        partners = [other] + [peer("z", s)[1] for s in range(1, nz)]
        for s in range(1, nx * ny):
            partners.append((section, at["z"] * nx * ny + lax.rem(at["y"] * nx + at["x"] + s, nx * ny)))
        for partner in partners:
            pl.semaphore_signal(barrier, inc=1, device_id=partner, device_id_type=MESH)
        pl.semaphore_wait(barrier, len(partners))

        def remote(source, target, send, receive, device):
            return pltpu.make_async_remote_copy(
                src_ref=source, dst_ref=target, send_sem=send, recv_sem=receive,
                device_id=device, device_id_type=MESH,
            )

        def cross_copy(m):
            return remote(snd, rcv.at[m], ssem.at[m], rsem.at[m], other)

        widths = {"x": nx, "y": ny, "z": nz}
        orders = {"A": "xyz", "B": "yxz"}
        landing = {"A": (rsx, rsy, rsz), "B": (rsa, rsb, rsc)}

        def reduce_phase(part, stage, g):
            axis = orders[part][stage]
            count = ra
            for later in orders[part][stage + 1 :]:
                count *= size[later]
            lanes = slice(0, adapt) if part == "A" else slice(adapt, 2 * adapt)
            copies = []
            base = 0 if part == "A" else 9
            for s in range(1, size[axis]):
                c, device = peer(axis, s)
                rows = rows_of(c * count, count)
                source = g.at[rows, lanes] if stage == 0 else landing[part][stage - 1].at[0, rows]
                i = base + 3 * stage + s - 1
                copies.append(remote(source, landing[part][stage].at[s - 1], gss.at[i], grs.at[i], device))
            return copies

        def reduce_sum(part, stage, g):
            axis = orders[part][stage]
            count = ra
            for later in orders[part][stage + 1 :]:
                count *= size[later]
            lanes = slice(0, adapt) if part == "A" else slice(adapt, 2 * adapt)
            rows = rows_of(at[axis] * count, count)
            mine = g[rows, lanes] if stage == 0 else landing[part][stage - 1][0, rows]
            total = mine.astype(F32)
            for s in range(size[axis] - 1):
                total = total + landing[part][stage][s].astype(F32)
            return total

        def place(d, part):
            z, y, x = d // (nx * ny), (d // nx) % ny, d % nx
            if part == "A":
                return ((x * ny + y) * nz + z) * ra
            return ((y * nx + x) * nz + z) * ra

        def write_grads(g, ybs, dfs, count):
            first = tdot(ybs, dz[:count])
            for d in range(dp):
                g[pl.ds(place(d, "A"), ra), 0:adapt] = first[d * ra : (d + 1) * ra].astype(BF)
            second = 4.0 * tdot(rb[:count], dfs)
            half = ra // 2
            for d in range(dp):
                block = second[d * half : (d + 1) * half].astype(BF)
                g[pl.ds(place(d, "B"), half), adapt : 2 * adapt] = block[:, :adapt]
                g[pl.ds(place(d, "B") + half, half), adapt : 2 * adapt] = block[:, adapt:]

        def all_start(g, stage):
            for part in "AB":
                for c in reduce_phase(part, stage, g):
                    c.start()

        def all_finish(g, stage):
            for part in "AB":
                for c in reduce_phase(part, stage, g):
                    c.wait()
                total = reduce_sum(part, stage, g)
                if stage < 2:
                    landing[part][stage][0] = total.astype(BF)
                elif part == "A":
                    ig_out[...] = total
                else:
                    half = ra // 2
                    og_out[:, 0:adapt] = total[:half]
                    og_out[:, adapt : 2 * adapt] = total[half:]

        plane = nx * ny
        piece = small_rows * features // (16 * plane)
        across = features // piece
        seat = at["y"] * nx + at["x"]

        def plane_peer(s):
            i = lax.rem(seat + s, plane)
            return i, (section, at["z"] * plane + i)

        def small_at(ref, i):
            return ref.at[rows_of((i // across) * 16, 16), rows_of(lax.rem(i, across) * piece, piece)]

        def small_scatter():
            copies = []
            for s in range(1, plane):
                i, device = plane_peer(s)
                copies.append(remote(small_at(small, i), small_in.at[s - 1], mss.at[s - 1], mrs.at[s - 1], device))
            return copies

        def small_along():
            n = plane - 1
            return [
                remote(small_mid, small_z.at[s - 1], mss.at[n + s - 1], mrs.at[n + s - 1], peer("z", s)[1])
                for s in range(1, nz)
            ]

        def small_gather():
            n = plane - 1 + nz - 1
            copies = []
            for s in range(1, plane):
                device = plane_peer(s)[1]
                copies.append(
                    remote(small_end, small_at(small_all, seat), mss.at[n + s - 1], mrs.at[n + s - 1], device)
                )
            return copies

        def small_begin():
            small[0:PRE_PAD] = pre_sum[0].astype(BF)
            small[PRE_PAD : 2 * PRE_PAD] = pre_sum[1].astype(BF)
            small[PRE : PRE + 1] = ob_sum[...].astype(BF)
            small[PRE_PAD + PRE : PRE_PAD + PRE + 1, 0:adapt] = ib_sum[...].astype(BF)
            for c in small_scatter():
                c.start()

        def small_middle():
            for c in small_scatter():
                c.wait()
            total = small_at(small, seat)[...].astype(F32)
            for s in range(plane - 1):
                total = total + small_in[s].astype(F32)
            small_mid[...] = total.astype(BF)
            for c in small_along():
                c.start()

        def small_late():
            for c in small_along():
                c.wait()
            total = small_mid[...].astype(F32)
            for s in range(nz - 1):
                total = total + small_z[s].astype(F32)
            small_end[...] = total.astype(BF)
            small_at(small_all, seat)[...] = small_end[...]
            for c in small_gather():
                c.start()

        def small_finish():
            for c in small_gather():
                c.wait()
            sm_out[...] = small_all[...].astype(F32)

        blocks = {}
        for b in range(3):
            blocks[b] = (ai.at[0, :, pl.ds(b * features, features)], w.at[b])
        blocks[3] = (ao.at[0], w.at[3])
        for c in range(chunks):
            blocks[4 + c] = (fi.at[0, :, pl.ds(c * features, features)], w.at[4 + c])
            blocks[8 + c] = (fo.at[0, pl.ds(c * features, features), :], w.at[8 + c])
        blocks[12] = (cq, w.at[12])
        blocks[13] = (cp.at[:, pl.ds(0, features)], w.at[13])
        blocks[14] = (cp.at[:, pl.ds(features, features)], w.at[14])
        blocks[15] = (co, w.at[15])
        blocks[16] = (di.at[0], wdi)
        blocks[17] = (do.at[0], wdo)

        def fetch(b):
            return pltpu.make_async_copy(blocks[b][0], blocks[b][1], wsem.at[b])

        def gain(i):
            return gains[0, i : i + 1, :].astype(F32)

        def prefix_setup(tokens):
            pad = jnp.zeros((PRE_PAD, features), BF)
            for m in range(2):
                k[m, pl.ds(tokens, PRE_PAD)] = pad
                v[m, pl.ds(tokens, PRE_PAD)] = pad
                k[m, pl.ds(tokens, PRE)] = prefix[:, 0, :]
                v[m, pl.ds(tokens, PRE)] = prefix[:, 1, :]
            ktp[...] = k[0, pl.ds(tokens, PRE_PAD)].T
            vtp[...] = v[0, pl.ds(tokens, PRE_PAD)].T
            pre_sum[...] = jnp.zeros_like(pre_sum)
            ib_sum[...] = jnp.zeros_like(ib_sum)
            ob_sum[...] = jnp.zeros_like(ob_sum)

        def project(rows, x, q, m):
            q[...] = (dot(x[...], w[0]) * 0.125).astype(BF)
            keys = dot(x[...], w[1]).astype(BF)
            k[m, 0:rows] = keys
            kt[m, :, 0:rows] = keys.T
            values = dot(x[...], w[2]).astype(BF)
            v[m, 0:rows] = values
            tt[:, 0:rows] = values.T

        def branch(rows, yb, slope, m, wait):
            if wait is not None:
                wait(16)
            pre = dot(yb[...], wdi[...]) + bi[...].astype(F32)
            act, turn = gelu_and_slope(pre)
            act = act.astype(BF)
            rb[pl.ds(m * rows, rows)] = act
            sa[m, 0:rows] = turn.astype(BF)
            if wait is not None:
                wait(17)
            f1[0:rows] = f1[0:rows] + 4.0 * (dot(act, wdo[...]) + bo[...].astype(F32))

            def step(c, carry):
                if wait is not None:
                    wait(4 + c)
                act, turn = gelu_and_slope(dot(yb[...], w[4 + c]))
                slope[1](c, turn.astype(BF))
                if wait is not None:
                    wait(8 + c)
                f1[0:rows] = f1[0:rows] + dot(act.astype(BF), w[8 + c])
                return carry

            if wait is not None:
                for c in range(chunks):
                    step(c, 0)
            else:
                lax.fori_loop(0, chunks, step, 0)

        def branch_back_adapter(rows, df, m):
            low = df[...]
            ob_sum[...] = ob_sum[...] + 4.0 * jnp.sum(low.astype(F32), axis=0, keepdims=True)
            grad = ((4.0 * dot_t(low, wdo[...])) * sa[m, 0:rows].astype(F32)).astype(BF)
            dz[pl.ds(m * rows, rows)] = grad
            ib_sum[...] = ib_sum[...] + jnp.sum(grad.astype(F32), axis=0, keepdims=True)

        def branch_back_feed(rows, df, slope, m):
            f1[0:rows] = f1[0:rows] + dot_t(dz[pl.ds(m * rows, rows)], wdi[...])

            def step(c, carry):
                grad = (dot_t(df[...], w[8 + c]) * slope[0](c).astype(F32)).astype(BF)
                f1[0:rows] = f1[0:rows] + dot_t(grad, w[4 + c])
                return carry

            lax.fori_loop(0, chunks, step, 0)

        def self_back(rows, m, q):
            def norm(r):
                dt = norm_back(f1[r], xh1[m, r].astype(F32), r1[m, r], gain(0))
                f1[r] = dt
                dqkv[0, r] = dt.astype(BF)

            by_rows(rows, norm)
            ot_rows = dot_t(dqkv[0, 0:rows], w[3]).astype(BF)
            dqkv[0, 0:rows] = ot_rows
            attend_back(
                rows, rows, True, pairs, dqkv.at[0, pl.ds(0, rows)], q,
                k.at[m, pl.ds(0, rows + PRE_PAD)], v.at[m, pl.ds(0, rows + PRE_PAD)],
                kt.at[m, :, pl.ds(0, rows)], ktp,
                lambda p: pw.at[m, p, pl.ds(0, rows + PRE_PAD), pl.ds(0, 2 * rows)],
                ot.at[:, pl.ds(0, rows)], dqkv.at[1, pl.ds(0, rows)], dqkv.at[2, pl.ds(0, rows)], pre_sum,
            )
            dqkv[0, 0:rows] = ot[:, 0:rows].T

        def self_input(rows, out):
            total = f1[0:rows]
            for b in range(3):
                total = total + dot_t(dqkv[b, 0:rows], w[b])
            out[...] = total.astype(BF)

        def encoder():
            R = src_rows

            def xin(m):
                return w.at[15, pl.ds(512 + m * R, R)]

            def q(m):
                return w.at[15, pl.ds(m * R, R)]

            def yb(m):
                return w.at[14, pl.ds(m * R, R)]

            def df(m):
                return w.at[14, pl.ds(512 + m * R, R)]

            def slope(m):
                def put(c, value):
                    w[12 + m, rows_of(c * R, R)] = value

                return (lambda c: w[12 + m, rows_of(c * R, R)]), put

            def load_x(m):
                return pltpu.make_async_copy(src.at[m], xin(m), xsem.at[m])

            load_x(0).start()
            for b in (0, 1, 2):
                fetch(b).start()
            load_x(1).start()
            prefix_setup(R)

            def forward(m):
                wait = (lambda b: fetch(b).wait()) if m == 0 else None
                load_x(m).wait()
                if wait is not None:
                    wait(0)
                    for b in (3, 16, 17, 4, 8):
                        fetch(b).start()
                    wait(1)
                    wait(2)
                    for b in (5, 9, 6, 10, 7, 11):
                        fetch(b).start()
                project(R, xin(m), q(m), m)
                key = lax.broadcasted_iota(jnp.int32, (enc_keys, PAIR), 0)
                seen = (key < sl[m]) | ((key >= R) & (key < R + PRE))
                bias[...] = jnp.where(seen, 0.0, NEG)
                attend(
                    R, R, True, pairs, q(m), k.at[m], tt, vtp, lambda p: pw.at[m, p], bias, ot,
                )
                if wait is not None:
                    wait(3)
                f1[...] = xin(m)[...].astype(F32) + dot(ot[...].T, w[3])

                def norm(r):
                    shaped, factor = norm_of(f1[r])
                    xh1[m, r] = shaped.astype(BF)
                    r1[m, r] = factor
                    h = shaped * gain(0)
                    f1[r] = h
                    yb(m)[r] = h.astype(BF)

                by_rows(R, norm)
                branch(R, yb(m), slope(m), m, wait)

                if m == 1:
                    cross_copy(0).wait_send()

                def last(r):
                    shaped, factor = norm_of(f1[r])
                    xh2[m, r] = shaped.astype(BF)
                    r2[m, r] = factor
                    snd[r] = (shaped * gain(1)).astype(BF)

                by_rows(R, last)
                cross_copy(m).start()

            def backward(m):
                if m == 0:
                    cross_copy(1).wait_send()
                cross_copy(m).wait_recv()

                def norm(r):
                    dt = norm_back(rcv[m, r].astype(F32), xh2[m, r].astype(F32), r2[m, r], gain(1))
                    f1[r] = dt
                    df(m)[r] = dt.astype(BF)

                by_rows(R, norm)
                branch_back_adapter(R, df(m), m)
                g = w.at[12]
                if m == 1:
                    write_grads(g, w[14, 0 : 2 * R], w[14, 512 : 512 + 2 * R], 2 * R)
                    all_start(g, 0)
                branch_back_feed(R, df(m), slope(m), m)
                if m == 1:
                    all_finish(g, 0)
                    all_start(g, 1)
                self_back(R, m, q(m))
                if m == 1:
                    small_begin()
                    all_finish(g, 1)
                    all_start(g, 2)
                self_input(R, xin(m))
                store_x(m).start()

            def store_x(m):
                return pltpu.make_async_copy(xin(m), tok.at[0, m], osem.at[m])

            forward(0)
            forward(1)
            backward(0)
            backward(1)
            small_middle()
            all_finish(w.at[12], 2)
            small_late()
            store_x(0).wait()
            store_x(1).wait()
            small_finish()

        def decoder():
            R = tgt_rows

            def shifted(r):
                return pl.ds(pl.multiple_of(r.start + R, LN_ROWS), LN_ROWS)

            def load_t(m):
                return pltpu.make_async_copy(tgt.at[m], dxin.at[m], xsem.at[m])

            def load_c(m):
                return pltpu.make_async_copy(ct.at[m], dct.at[m], xsem.at[2 + m])

            load_t(0).start()
            for b in [0, 1, 2]:
                fetch(b).start()
            load_t(1).start()
            for b in [3, 12, 13, 14, 15, 16, 17, 4, 8, 5, 9, 6, 10, 7, 11]:
                fetch(b).start()
            load_c(0).start()
            load_c(1).start()
            prefix_setup(R)

            def pick(c):
                parts = [pw[1, 2 * c + i // 2, pl.ds((i % 2) * R, R), 256:512] for i in range(4)]
                return jnp.concatenate(parts, axis=1)

            def put(c, value):
                for i in range(4):
                    pw[1, 2 * c + i // 2, pl.ds((i % 2) * R, R), 256:512] = value[:, 256 * i : 256 * (i + 1)]

            slope = (pick, put)

            def early(m):
                return f1.at[pl.ds(R, R)] if m == 0 else da

            def dq_(m):
                return k.at[m, pl.ds(dec_keys, R)]

            def dqc_(m):
                return v.at[m, pl.ds(dec_keys, R)]

            def self_probs(m):
                return lambda p: pw.at[m, p, pl.ds(0, dec_keys), pl.ds(0, 2 * R)]

            def cross_probs():
                return lambda p: pw.at[0, p, pl.ds(0, src_rows), pl.ds(2 * R, 2 * R)]

            def self_forward(m):
                load_t(m).wait()
                if m == 0:
                    for b in range(3):
                        fetch(b).wait()
                project(R, dxin.at[m], dq_(m), m)
                key = lax.broadcasted_iota(jnp.int32, (dec_keys, PAIR), 0)
                query = lax.broadcasted_iota(jnp.int32, (dec_keys, PAIR), 1)
                seen = (key <= query) | ((key >= R) & (key < R + PRE))
                bias[0:dec_keys] = jnp.where(seen, 0.0, NEG)
                attend(
                    R, R, True, pairs, dq_(m), k.at[m, pl.ds(0, dec_keys)],
                    tt.at[:, pl.ds(0, R)], vtp, self_probs(m), bias.at[pl.ds(0, dec_keys)],
                    ot.at[:, pl.ds(0, R)],
                )
                if m == 0:
                    fetch(3).wait()
                f1[0:R] = dxin[m].astype(F32) + dot(ot[:, 0:R].T, w[3])

                def norm(r):
                    shaped, factor = norm_of(f1[r])
                    xh1[m, r] = shaped.astype(BF)
                    r1[m, r] = factor
                    h = shaped * gain(0)
                    early(m)[r] = h
                    xh1[m, shifted(r)] = h.astype(BF)

                by_rows(R, norm)
                if m == 0:
                    fetch(12).wait()
                dqc_(m)[...] = (dot(xh1[m, R : 2 * R], w[12]) * 0.125).astype(BF)

            def middle(m):
                cross_copy(m).wait_recv()
                if m == 0:
                    fetch(13).wait()
                    fetch(14).wait()
                keys = dot(rcv[m], w[13]).astype(BF)
                kc[...] = keys
                kct[...] = keys.T
                values = dot(rcv[m], w[14]).astype(BF)
                vc[...] = values
                tt[...] = values.T
                key = lax.broadcasted_iota(jnp.int32, (src_rows, PAIR), 0)
                bias[0:src_rows] = jnp.where(key < sl[m], 0.0, NEG)
                attend(
                    R, src_rows, False, pairs, dqc_(m), kc, tt, None, cross_probs(),
                    bias.at[pl.ds(0, src_rows)], ot.at[:, pl.ds(0, R)],
                )
                if m == 0:
                    fetch(15).wait()
                f1[0:R] = early(m)[...] + dot(ot[:, 0:R].T, w[15])
                yb = xh1.at[m, pl.ds(R, R)]

                def norm(r):
                    shaped, factor = norm_of(f1[r])
                    xh2[m, r] = shaped.astype(BF)
                    r2[m, r] = factor
                    h = shaped * gain(1)
                    f1[r] = h
                    yb[r] = h.astype(BF)

                by_rows(R, norm)
                branch(R, yb, slope, m, (lambda b: fetch(b).wait()) if m == 0 else None)
                if m == 0:
                    load_c(0).wait()
                    load_c(1).wait()
                df = xh2.at[m, pl.ds(R, R)]

                def turn(r):
                    shaped, factor = norm_of(f1[r])
                    row = lax.broadcasted_iota(jnp.int32, (LN_ROWS, 1), 0) + r.start
                    on = jnp.where(row < tl[m], 1.0, 0.0)
                    grad = dct[m, r].astype(F32) * on
                    dct[m, r] = (shaped * gain(2) * on).astype(BF)
                    dt = norm_back(grad, shaped, factor, gain(2))
                    f1[r] = dt
                    df[r] = dt.astype(BF)

                by_rows(R, turn)
                store_d(m).start()
                branch_back_adapter(R, df, m)
                branch_back_feed(R, df, slope, m)
                if m == 1:
                    write_grads(
                        g, xh1[:, R : 2 * R].reshape(2 * R, features), xh2[:, R : 2 * R].reshape(2 * R, features), 2 * R
                    )
                    all_start(g, 0)

                def back(r):
                    dt = norm_back(f1[r], xh2[m, r].astype(F32), r2[m, r], gain(1))
                    f1[r] = dt
                    dqkv[0, r] = dt.astype(BF)

                by_rows(R, back)
                grad_mixed = dot_t(dqkv[0, 0:R], w[15]).astype(BF)
                dqkv[0, 0:R] = grad_mixed
                attend_back(
                    R, src_rows, False, pairs, dqkv.at[0, pl.ds(0, R)], dqc_(m), kc, vc, kct, None,
                    cross_probs(), ot.at[:, pl.ds(0, R)], dqkv.at[1], dqkv.at[2], None,
                )
                if m == 1:
                    cross_copy(0).wait_send()
                snd[...] = (dot_t(dqkv[1], w[13]) + dot_t(dqkv[2], w[14])).astype(BF)
                cross_copy(m).start()
                early(m)[...] = f1[0:R] + dot_t(ot[:, 0:R].T, w[12])

            def store_d(m):
                return pltpu.make_async_copy(dct.at[m], tok.at[0, m, pl.ds(0, R)], osem.at[m])

            def store_y(m):
                return pltpu.make_async_copy(dxin.at[m], tok.at[0, m, pl.ds(R, R)], osem.at[2 + m])

            g = w.at[8]
            self_forward(0)
            self_forward(1)
            middle(0)
            middle(1)
            all_finish(g, 0)
            all_start(g, 1)
            for m in range(2):
                f1[0:R] = early(m)[...]
                self_back(R, m, dq_(m))
                if m == 0:
                    self_input(R, dxin.at[m])
                    store_y(m).start()
                    all_finish(g, 1)
                    all_start(g, 2)
            small_begin()
            self_input(R, dxin.at[1])
            store_y(1).start()
            small_middle()
            all_finish(g, 2)
            small_late()
            for m in range(2):
                store_d(m).wait()
                store_y(m).wait()
            cross_copy(1).wait_send()
            small_finish()

        pl.when(section == 0)(encoder)
        pl.when(section == 1)(decoder)

    vm = pltpu.VMEM
    plane = nx * ny
    piece = small_rows * features // (16 * plane)
    smalls = 2 * (plane - 1) + nz - 1
    scratch = [
        vm((16, features, features), BF),
        vm((features, adapt), BF),
        vm((adapt, features), BF),
        vm((2, pairs, enc_keys, 2 * src_rows), BF),
        vm((2, enc_keys, features), BF),
        vm((2, enc_keys, features), BF),
        vm((2, features, src_rows), BF),
        vm((features, src_rows), BF),
        vm((features, src_rows), BF),
        vm((features, PRE_PAD), BF),
        vm((features, PRE_PAD), BF),
        vm((2, src_rows, features), BF),
        vm((2, src_rows, features), BF),
        vm((2, src_rows, 1), F32),
        vm((2, src_rows, 1), F32),
        vm((2, src_rows, adapt), BF),
        vm((2 * src_rows, adapt), BF),
        vm((2 * src_rows, adapt), BF),
        vm((src_rows, features), BF),
        vm((2, src_rows, features), BF),
        vm((src_rows, features), F32),
        vm((3, src_rows, features), BF),
        vm((nx - 1, ny * nz * ra, adapt), BF),
        vm((ny - 1, nz * ra, adapt), BF),
        vm((nz - 1, ra, adapt), BF),
        vm((ny - 1, nx * nz * ra, adapt), BF),
        vm((nx - 1, nz * ra, adapt), BF),
        vm((nz - 1, ra, adapt), BF),
        vm((2, PRE_PAD, features), F32),
        vm((enc_keys, PAIR), F32),
        vm((1, adapt), F32),
        vm((1, features), F32),
        vm((small_rows, features), BF),
        vm((plane - 1, 16, piece), BF),
        vm((16, piece), BF),
        vm((nz - 1, 16, piece), BF),
        vm((16, piece), BF),
        vm((small_rows, features), BF),
        vm((2, tgt_rows, features), BF),
        vm((2, tgt_rows, features), BF),
        vm((tgt_rows, features), F32),
        vm((src_rows, features), BF),
        vm((src_rows, features), BF),
        vm((features, src_rows), BF),
        pltpu.SemaphoreType.DMA((18,)),
        pltpu.SemaphoreType.DMA((4,)),
        pltpu.SemaphoreType.DMA((4,)),
        pltpu.SemaphoreType.DMA((2,)),
        pltpu.SemaphoreType.DMA((2,)),
        pltpu.SemaphoreType.DMA((18,)),
        pltpu.SemaphoreType.DMA((18,)),
        pltpu.SemaphoreType.DMA((smalls,)),
        pltpu.SemaphoreType.DMA((smalls,)),
    ]
    return kernel, scratch, ra


def finish(tok, ig, og, small, tok_out, pre_out, ig_out, og_out, ib_out, ob_out, sem):
    copy = pltpu.make_async_copy(tok, tok_out, sem)
    copy.start()
    adapt = ig.shape[1]
    pre_out[:, 0, :] = small[0:PRE]
    pre_out[:, 1, :] = small[PRE_PAD : PRE_PAD + PRE]
    ig_out[0] = ig[...]
    og_out[0] = og[...]
    ob_out[...] = small[PRE : PRE + 1]
    ib_out[...] = small[PRE_PAD + PRE : PRE_PAD + PRE + 1, 0:adapt]
    copy.wait()


def solution(mesh):
    dp = mesh.shape["dp"]
    nz = 4
    nx = math.isqrt(dp // nz)
    ny = dp // (nz * nx)

    def per_device(
        source, target, cotangent, source_lengths, target_lengths, attention_in, attention_out,
        cross_query, cross_pair, cross_output, feed_in, feed_out, adapter_in, adapter_in_bias,
        adapter_out, adapter_out_bias, prefix, norm_gains,
    ):
        features = source.shape[2]
        adapt = adapter_in.shape[2]
        kernel, scratch, ra = make_kernel(
            nz, ny, nx, features, feed_in.shape[2], adapt, source.shape[1], target.shape[1]
        )
        anywhere = pl.BlockSpec(memory_space=pl.ANY)
        scalar = pl.BlockSpec(memory_space=pltpu.SMEM)
        vector = pl.BlockSpec(memory_space=pltpu.VMEM)
        tok, ig, og, small = pl.pallas_call(
            kernel,
            out_shape=(
                jax.ShapeDtypeStruct((1, source.shape[0], source.shape[1], features), BF),
                jax.ShapeDtypeStruct((ra, adapt), F32),
                jax.ShapeDtypeStruct((ra // 2, features), F32),
                jax.ShapeDtypeStruct((2 * PRE_PAD, features), F32),
            ),
            in_specs=[anywhere] * 3 + [scalar] * 2 + [anywhere] * 9 + [vector] * 4,
            out_specs=(anywhere, vector, vector, vector),
            scratch_shapes=scratch,
            compiler_params=pltpu.CompilerParams(
                collective_id=0, has_side_effects=True, vmem_limit_bytes=67000000
            ),
        )(
            source, target, cotangent, source_lengths.reshape(-1), target_lengths.reshape(-1), attention_in,
            attention_out, cross_query, cross_pair, cross_output, feed_in, feed_out, adapter_in, adapter_out,
            adapter_in_bias, adapter_out_bias, prefix[0].transpose(1, 0, 2), norm_gains,
        )
        tok, pre, ig, og, ib, ob = pl.pallas_call(
            finish,
            out_shape=(
                jax.ShapeDtypeStruct(tok.shape, BF),
                jax.ShapeDtypeStruct((PRE, 2, features), F32),
                jax.ShapeDtypeStruct((1, ra, adapt), F32),
                jax.ShapeDtypeStruct((1, ra // 2, features), F32),
                jax.ShapeDtypeStruct((1, adapt), F32),
                jax.ShapeDtypeStruct((1, features), F32),
            ),
            in_specs=[anywhere, vector, vector, vector],
            out_specs=(vector, vector, vector, vector, vector, vector),
            scratch_shapes=[pltpu.SemaphoreType.DMA(())],
        )(tok, ig, og, small)
        return tok, pre.transpose(1, 0, 2)[None], ig, og, ib, ob

    return jax.shard_map(
        per_device,
        mesh=mesh,
        in_specs=(
            P(None, "dp", None),
            P(None, "dp", None),
            P(None, "dp", None),
            P(None, "dp"),
            P(None, "dp"),
            P("section", None, None),
            P("section", None, None),
            P(),
            P(),
            P(),
            P("section", None, None),
            P("section", None, None),
            P("section", None, None),
            P("section", None),
            P("section", None, None),
            P("section", None),
            P("section", None, None, None),
            P("section", None, None),
        ),
        out_specs=(
            P("section", None, "dp", None),
            P("section", None, None, None),
            P("section", "dp", None),
            P("section", "dp", None),
            P("section", None),
            P("section", None),
        ),
        check_vma=False,
    )
```

profile of v0, /device:TPU:0, one launch (start us, length us, event | category | flops | bytes accessed | tf_op | source)
XLA Modules:
  0.0 134.4 jit_solution(2125363133880703550)
XLA Ops:
  0.6 130.0 %shard_map.217 = (bf16[1,2,256,1024]{3,2,1,0:T(8,128)(2,1)}, f32[64,512]{1,0:T(8,128)}, f32[32,1024]{1,0:T(8,128)}, f32[64,1024]{1,0:T(8,128)}) custom-call(bf16[2,256,1024]{2,1,0:T(8,128)(2,1)} %src.1, bf16[2,128,1024]{2,1,0:T(8,128)(2,1)} %tgt.1, bf16[2,128,1024]{2,1,0:T(8,128)(2,1)} %ct.1, s32[2]{0:T(128)} %bitcast.9, s32[2]{0:T(128)} %bitcast.10, ...), custom_call_target="tpu_custom_call" | custom-call | tf_op jit(solution)/shard_map/pallas_call | solution.py:818
  130.7 3.4 %shard_map.218 = (bf16[1,2,256,1024]{3,2,1,0:T(8,128)(2,1)}, f32[30,2,1024]{2,1,0:T(2,128)}, f32[1,64,512]{2,1,0:T(8,128)}, f32[1,32,1024]{2,1,0:T(8,128)}, f32[1,512]{1,0:T(1,128)}, /*index=5*/f32[1,1024]{1,0:T(1,128)}) custom-call(bf16[1,2,256,1024]{3,2,1,0:T(8,128)(2,1)} %get-tuple-element.16.tok, f32[64,512]{1,0:T(8,128)} %get-tuple-element.17.ig, ...), custom_call_target="tpu_custom_call" | custom-call | tf_op jit(solution)/shard_map/pallas_call | solution.py:837
where the time goes:
time: 133 us; the launch traced here: 134 us
  Pallas kernels  133 us (100%)
    pallas_call x1, Pallas kernels, per_device(): pl.pallas_call(kernel, out_shape=(jax.ShapeDtypeStruct((1, source.shape[0...  130 us
    pallas_call x1, Pallas kernels, per_device(): pl.pallas_call(finish, out_shape=(jax.ShapeDtypeStruct(tok.shape, BF), ja...  3.45 us

commit v1 on v0

--- a/solution.py
+++ b/solution.py
@@ -18,7 +18,12 @@
 PRE_PAD = 32
 PAIR = 128
 HALF = 64
-LN_ROWS = 64
+LN_ROWS = 128
+ENC_PAIRS = 4
+SELF_PAIRS = 2
+CROSS_PAIRS = 8
+ENC_CHUNKS = 1
+DEC_CHUNKS = 4
 
 
 def dot(a, b):
@@ -68,7 +73,7 @@
     return jnp.concatenate([jnp.where(first, block, zero), jnp.where(first, zero, block)], axis=0)
 
 
-def attend(rows, tokens, prefixed, pairs, q, k, vt, vtp, probs, bias, out_t):
+def attend(unroll, rows, tokens, prefixed, pairs, q, k, vt, vtp, probs, bias, out_t):
     def step(p, carry):
         lanes = rows_of(p * PAIR, PAIR)
         scores = dot_t(k[:, lanes], both_heads(q[:, lanes]))
@@ -86,10 +91,10 @@
             out_t[head, :] = mixed.astype(BF)
         return carry
 
-    lax.fori_loop(0, pairs, step, 0, unroll=4)
-
-
-def attend_back(rows, tokens, prefixed, pairs, grad, q, k, v, kt, ktp, probs, dq_t, dk, dv, pre_sum):
+    lax.fori_loop(0, pairs, step, 0, unroll=unroll)
+
+
+def attend_back(unroll, rows, tokens, prefixed, pairs, grad, q, k, v, kt, ktp, probs, dq_t, dk, dv, pre_sum):
     def step(p, carry):
         lanes = rows_of(p * PAIR, PAIR)
         grads = both_heads(grad[:, lanes])
@@ -115,7 +120,7 @@
             dq_t[head, :] = (back * 0.125).astype(BF)
         return carry
 
-    lax.fori_loop(0, pairs, step, 0, unroll=4)
+    lax.fori_loop(0, pairs, step, 0, unroll=unroll)
 
 
 def make_kernel(nz, ny, nx, features, hidden, adapt, src_rows, tgt_rows):
@@ -147,22 +152,28 @@
             return c[axis], (section, (c["z"] * ny + c["y"]) * nx + c["x"])
 
         other = (1 - section, here)
-        barrier = pltpu.get_barrier_semaphore()
-        partners = [other] + [peer("z", s)[1] for s in range(1, nz)]
-        for s in range(1, nx * ny):
-            partners.append((section, at["z"] * nx * ny + lax.rem(at["y"] * nx + at["x"] + s, nx * ny)))
-        for partner in partners:
-            pl.semaphore_signal(barrier, inc=1, device_id=partner, device_id_type=MESH)
-        pl.semaphore_wait(barrier, len(partners))
-
         def remote(source, target, send, receive, device):
             return pltpu.make_async_remote_copy(
                 src_ref=source, dst_ref=target, send_sem=send, recv_sem=receive,
                 device_id=device, device_id_type=MESH,
             )
 
-        def cross_copy(m):
-            return remote(snd, rcv.at[m], ssem.at[m], rsem.at[m], other)
+        def memory_copy(m, i):
+            rows = rows_of(i * PAIR, PAIR)
+            return remote(snd.at[rows], rcv.at[m, rows], ssem.at[2 * m + i], rsem.at[2 * m + i], other)
+
+        def back_copy(m, i):
+            lanes = pl.ds(i * (features // 2), features // 2)
+            return remote(snd.at[:, lanes], rcv.at[m, :, lanes], ssem.at[2 * m + i], rsem.at[2 * m + i], other)
+
+        def greet():
+            barrier = pltpu.get_barrier_semaphore()
+            partners = [other] + [peer("z", s)[1] for s in range(1, nz)]
+            for s in range(1, nx * ny):
+                partners.append((section, at["z"] * nx * ny + lax.rem(at["y"] * nx + at["x"] + s, nx * ny)))
+            for partner in partners:
+                pl.semaphore_signal(barrier, inc=1, device_id=partner, device_id_type=MESH)
+            pl.semaphore_wait(barrier, len(partners))
 
         widths = {"x": nx, "y": ny, "z": nz}
         orders = {"A": "xyz", "B": "yxz"}
@@ -198,21 +209,33 @@
             return total
 
         def place(d, part):
-            z, y, x = d // (nx * ny), (d // nx) % ny, d % nx
+            z, y, x = lax.div(d, nx * ny), lax.rem(lax.div(d, nx), ny), lax.rem(d, nx)
             if part == "A":
-                return ((x * ny + y) * nz + z) * ra
-            return ((y * nx + x) * nz + z) * ra
+                return pl.multiple_of(((x * ny + y) * nz + z) * ra, ra)
+            return pl.multiple_of(((y * nx + x) * nz + z) * ra, ra)
 
         def write_grads(g, ybs, dfs, count):
-            first = tdot(ybs, dz[:count])
-            for d in range(dp):
-                g[pl.ds(place(d, "A"), ra), 0:adapt] = first[d * ra : (d + 1) * ra].astype(BF)
-            second = 4.0 * tdot(rb[:count], dfs)
+            group = 2 * PAIR
             half = ra // 2
-            for d in range(dp):
-                block = second[d * half : (d + 1) * half].astype(BF)
-                g[pl.ds(place(d, "B"), half), adapt : 2 * adapt] = block[:, :adapt]
-                g[pl.ds(place(d, "B") + half, half), adapt : 2 * adapt] = block[:, adapt:]
+
+            def first(t, carry):
+                block = tdot(ybs(rows_of(t * group, group)), dz[0:count])
+                for i in range(group // ra):
+                    d = t * (group // ra) + i
+                    g[pl.ds(place(d, "A"), ra), 0:adapt] = block[i * ra : (i + 1) * ra].astype(BF)
+                return carry
+
+            def second(t, carry):
+                block = 4.0 * tdot(rb[0:count, rows_of(t * PAIR, PAIR)], dfs())
+                for i in range(PAIR // half):
+                    d = t * (PAIR // half) + i
+                    part = block[i * half : (i + 1) * half]
+                    part = jnp.concatenate([part[:, :adapt], part[:, adapt:]], axis=0)
+                    g[pl.ds(place(d, "B"), ra), adapt : 2 * adapt] = part.astype(BF)
+                return carry
+
+            lax.fori_loop(0, features // group, first, 0)
+            lax.fori_loop(0, adapt // PAIR, second, 0)
 
         def all_start(g, stage):
             for part in "AB":
@@ -317,6 +340,14 @@
         blocks[16] = (di.at[0], wdi)
         blocks[17] = (do.at[0], wdo)
 
+        def fetch_in(c):
+            lanes = rows_of(c * features, features)
+            return pltpu.make_async_copy(fi.at[0, :, lanes], w.at[4 + c], wsem.at[4 + c])
+
+        def fetch_out(c):
+            rows = rows_of(c * features, features)
+            return pltpu.make_async_copy(fo.at[0, rows, :], w.at[8 + c], wsem.at[8 + c])
+
         def fetch(b):
             return pltpu.make_async_copy(blocks[b][0], blocks[b][1], wsem.at[b])
 
@@ -345,52 +376,52 @@
             v[m, 0:rows] = values
             tt[:, 0:rows] = values.T
 
-        def branch(rows, yb, slope, m, wait):
-            if wait is not None:
-                wait(16)
+        def branch(unroll, rows, yb, slope, m):
+            @pl.when(m == 0)
+            def _():
+                fetch(16).wait()
+                fetch(17).wait()
+
             pre = dot(yb[...], wdi[...]) + bi[...].astype(F32)
             act, turn = gelu_and_slope(pre)
             act = act.astype(BF)
-            rb[pl.ds(m * rows, rows)] = act
+            rb[rows_of(m * rows, rows)] = act
             sa[m, 0:rows] = turn.astype(BF)
-            if wait is not None:
-                wait(17)
             f1[0:rows] = f1[0:rows] + 4.0 * (dot(act, wdo[...]) + bo[...].astype(F32))
 
             def step(c, carry):
-                if wait is not None:
-                    wait(4 + c)
+                @pl.when(m == 0)
+                def _():
+                    if rows == src_rows:
+                        fetch_in(c).wait()
+                    fetch_out(c).wait()
+
                 act, turn = gelu_and_slope(dot(yb[...], w[4 + c]))
                 slope[1](c, turn.astype(BF))
-                if wait is not None:
-                    wait(8 + c)
                 f1[0:rows] = f1[0:rows] + dot(act.astype(BF), w[8 + c])
                 return carry
 
-            if wait is not None:
-                for c in range(chunks):
-                    step(c, 0)
-            else:
-                lax.fori_loop(0, chunks, step, 0)
+            lax.fori_loop(0, chunks, step, 0, unroll=unroll)
 
         def branch_back_adapter(rows, df, m):
             low = df[...]
             ob_sum[...] = ob_sum[...] + 4.0 * jnp.sum(low.astype(F32), axis=0, keepdims=True)
             grad = ((4.0 * dot_t(low, wdo[...])) * sa[m, 0:rows].astype(F32)).astype(BF)
-            dz[pl.ds(m * rows, rows)] = grad
+            dz[rows_of(m * rows, rows)] = grad
             ib_sum[...] = ib_sum[...] + jnp.sum(grad.astype(F32), axis=0, keepdims=True)
 
-        def branch_back_feed(rows, df, slope, m):
-            f1[0:rows] = f1[0:rows] + dot_t(dz[pl.ds(m * rows, rows)], wdi[...])
+        def branch_back_feed(unroll, rows, df, slope, m, turned):
+            f1[0:rows] = f1[0:rows] + dot_t(dz[rows_of(m * rows, rows)], wdi[...])
 
             def step(c, carry):
                 grad = (dot_t(df[...], w[8 + c]) * slope[0](c).astype(F32)).astype(BF)
-                f1[0:rows] = f1[0:rows] + dot_t(grad, w[4 + c])
+                back = dot(grad, w[c]) if turned else dot_t(grad, w[4 + c])
+                f1[0:rows] = f1[0:rows] + back
                 return carry
 
-            lax.fori_loop(0, chunks, step, 0)
-
-        def self_back(rows, m, q):
+            lax.fori_loop(0, chunks, step, 0, unroll=unroll)
+
+        def self_back(unroll, rows, m, q, between=None):
             def norm(r):
                 dt = norm_back(f1[r], xh1[m, r].astype(F32), r1[m, r], gain(0))
                 f1[r] = dt
@@ -399,8 +430,10 @@
             by_rows(rows, norm)
             ot_rows = dot_t(dqkv[0, 0:rows], w[3]).astype(BF)
             dqkv[0, 0:rows] = ot_rows
+            if between is not None:
+                between()
             attend_back(
-                rows, rows, True, pairs, dqkv.at[0, pl.ds(0, rows)], q,
+                unroll, rows, rows, True, pairs, dqkv.at[0, pl.ds(0, rows)], q,
                 k.at[m, pl.ds(0, rows + PRE_PAD)], v.at[m, pl.ds(0, rows + PRE_PAD)],
                 kt.at[m, :, pl.ds(0, rows)], ktp,
                 lambda p: pw.at[m, p, pl.ds(0, rows + PRE_PAD), pl.ds(0, 2 * rows)],
@@ -414,135 +447,32 @@
                 total = total + dot_t(dqkv[b, 0:rows], w[b])
             out[...] = total.astype(BF)
 
-        def encoder():
-            R = src_rows
-
-            def xin(m):
-                return w.at[15, pl.ds(512 + m * R, R)]
-
-            def q(m):
-                return w.at[15, pl.ds(m * R, R)]
-
-            def yb(m):
-                return w.at[14, pl.ds(m * R, R)]
-
-            def df(m):
-                return w.at[14, pl.ds(512 + m * R, R)]
-
-            def slope(m):
-                def put(c, value):
-                    w[12 + m, rows_of(c * R, R)] = value
-
-                return (lambda c: w[12 + m, rows_of(c * R, R)]), put
-
-            def load_x(m):
-                return pltpu.make_async_copy(src.at[m], xin(m), xsem.at[m])
-
+        def twice(body):
+            def step(m, carry):
+                body(m)
+                return carry
+
+            lax.fori_loop(0, 2, step, 0)
+
+        def xin(m):
+            return w.at[15, rows_of(512 + m * src_rows, src_rows)]
+
+        def load_x(m):
+            return pltpu.make_async_copy(src.at[m], xin(m), xsem.at[m])
+
+        def load_t(m):
+            return pltpu.make_async_copy(tgt.at[m], dxin.at[m], xsem.at[m])
+
+        def load_c(m):
+            return pltpu.make_async_copy(ct.at[m], dct.at[m], xsem.at[2 + m])
+
+        def encoder_loads():
             load_x(0).start()
             for b in (0, 1, 2):
                 fetch(b).start()
             load_x(1).start()
-            prefix_setup(R)
-
-            def forward(m):
-                wait = (lambda b: fetch(b).wait()) if m == 0 else None
-                load_x(m).wait()
-                if wait is not None:
-                    wait(0)
-                    for b in (3, 16, 17, 4, 8):
-                        fetch(b).start()
-                    wait(1)
-                    wait(2)
-                    for b in (5, 9, 6, 10, 7, 11):
-                        fetch(b).start()
-                project(R, xin(m), q(m), m)
-                key = lax.broadcasted_iota(jnp.int32, (enc_keys, PAIR), 0)
-                seen = (key < sl[m]) | ((key >= R) & (key < R + PRE))
-                bias[...] = jnp.where(seen, 0.0, NEG)
-                attend(
-                    R, R, True, pairs, q(m), k.at[m], tt, vtp, lambda p: pw.at[m, p], bias, ot,
-                )
-                if wait is not None:
-                    wait(3)
-                f1[...] = xin(m)[...].astype(F32) + dot(ot[...].T, w[3])
-
-                def norm(r):
-                    shaped, factor = norm_of(f1[r])
-                    xh1[m, r] = shaped.astype(BF)
-                    r1[m, r] = factor
-                    h = shaped * gain(0)
-                    f1[r] = h
-                    yb(m)[r] = h.astype(BF)
-
-                by_rows(R, norm)
-                branch(R, yb(m), slope(m), m, wait)
-
-                if m == 1:
-                    cross_copy(0).wait_send()
-
-                def last(r):
-                    shaped, factor = norm_of(f1[r])
-                    xh2[m, r] = shaped.astype(BF)
-                    r2[m, r] = factor
-                    snd[r] = (shaped * gain(1)).astype(BF)
-
-                by_rows(R, last)
-                cross_copy(m).start()
-
-            def backward(m):
-                if m == 0:
-                    cross_copy(1).wait_send()
-                cross_copy(m).wait_recv()
-
-                def norm(r):
-                    dt = norm_back(rcv[m, r].astype(F32), xh2[m, r].astype(F32), r2[m, r], gain(1))
-                    f1[r] = dt
-                    df(m)[r] = dt.astype(BF)
-
-                by_rows(R, norm)
-                branch_back_adapter(R, df(m), m)
-                g = w.at[12]
-                if m == 1:
-                    write_grads(g, w[14, 0 : 2 * R], w[14, 512 : 512 + 2 * R], 2 * R)
-                    all_start(g, 0)
-                branch_back_feed(R, df(m), slope(m), m)
-                if m == 1:
-                    all_finish(g, 0)
-                    all_start(g, 1)
-                self_back(R, m, q(m))
-                if m == 1:
-                    small_begin()
-                    all_finish(g, 1)
-                    all_start(g, 2)
-                self_input(R, xin(m))
-                store_x(m).start()
-
-            def store_x(m):
-                return pltpu.make_async_copy(xin(m), tok.at[0, m], osem.at[m])
-
-            forward(0)
-            forward(1)
-            backward(0)
-            backward(1)
-            small_middle()
-            all_finish(w.at[12], 2)
-            small_late()
-            store_x(0).wait()
-            store_x(1).wait()
-            small_finish()
-
-        def decoder():
-            R = tgt_rows
-
-            def shifted(r):
-                return pl.ds(pl.multiple_of(r.start + R, LN_ROWS), LN_ROWS)
-
-            def load_t(m):
-                return pltpu.make_async_copy(tgt.at[m], dxin.at[m], xsem.at[m])
-
-            def load_c(m):
-                return pltpu.make_async_copy(ct.at[m], dct.at[m], xsem.at[2 + m])
-
+
+        def decoder_loads():
             load_t(0).start()
             for b in [0, 1, 2]:
                 fetch(b).start()
@@ -551,7 +481,139 @@
                 fetch(b).start()
             load_c(0).start()
             load_c(1).start()
+
+        def encoder():
+            R = src_rows
+
+            def q(m):
+                return w.at[15, rows_of(m * R, R)]
+
+            def yb(m):
+                return w.at[14, rows_of(m * R, R)]
+
+            def df(m):
+                return w.at[14, rows_of(512 + m * R, R)]
+
+            def slope(m):
+                def put(c, value):
+                    w[12 + m, rows_of(c * R, R)] = value
+
+                return (lambda c: w[12 + m, rows_of(c * R, R)]), put
+
+            def forward(m):
+                load_x(m).wait()
+
+                @pl.when(m == 0)
+                def _():
+                    fetch(0).wait()
+                    for b in (3, 16, 17, 4, 8):
+                        fetch(b).start()
+                    fetch(1).wait()
+                    fetch(2).wait()
+                    for b in (5, 9, 6, 10, 7, 11):
+                        fetch(b).start()
+
+                project(R, xin(m), q(m), m)
+                key = lax.broadcasted_iota(jnp.int32, (enc_keys, PAIR), 0)
+                seen = (key < sl[m]) | ((key >= R) & (key < R + PRE))
+                bias[...] = jnp.where(seen, 0.0, NEG)
+                attend(
+                    ENC_PAIRS, R, R, True, pairs, q(m), k.at[m], tt, vtp, lambda p: pw.at[m, p], bias, ot,
+                )
+                pl.when(m == 0)(fetch(3).wait)
+                f1[...] = xin(m)[...].astype(F32) + dot(ot[...].T, w[3])
+
+                def norm(r):
+                    shaped, factor = norm_of(f1[r])
+                    xh1[m, r] = shaped.astype(BF)
+                    r1[m, r] = factor
+                    h = shaped * gain(0)
+                    f1[r] = h
+                    yb(m)[r] = h.astype(BF)
+
+                by_rows(R, norm)
+                branch(ENC_CHUNKS, R, yb(m), slope(m), m)
+
+
+                @pl.when(m == 1)
+                def _():
+                    for i in range(src_rows // PAIR):
+                        memory_copy(0, i).wait_send()
+
+                def last(r):
+                    shaped, factor = norm_of(f1[r])
+                    xh2[m, r] = shaped.astype(BF)
+                    r2[m, r] = factor
+                    snd[r] = (shaped * gain(1)).astype(BF)
+                    memory_copy(m, r.start // PAIR).start()
+
+                by_rows(R, last)
+
+            def backward(m):
+
+                @pl.when(m == 0)
+                def _():
+                    for i in range(src_rows // PAIR):
+                        memory_copy(1, i).wait_send()
+
+                back_copy(m, 0).wait_recv()
+                back_copy(m, 1).wait_recv()
+
+                def norm(r):
+                    dt = norm_back(rcv[m, r].astype(F32), xh2[m, r].astype(F32), r2[m, r], gain(1))
+                    f1[r] = dt
+                    df(m)[r] = dt.astype(BF)
+
+                by_rows(R, norm)
+                branch_back_adapter(R, df(m), m)
+                g = w.at[12]
+
+                @pl.when(m == 1)
+                def _():
+                    write_grads(g, lambda r: w[14, 0 : 2 * R, r], lambda: w[14, 512 : 512 + 2 * R], 2 * R)
+                    all_start(g, 0)
+
+                branch_back_feed(ENC_CHUNKS, R, df(m), slope(m), m, False)
+
+                def between():
+                    @pl.when(m == 1)
+                    def _():
+                        all_finish(g, 0)
+                        all_start(g, 1)
+
+                self_back(ENC_PAIRS, R, m, q(m), between)
+
+                @pl.when(m == 1)
+                def _():
+                    small_begin()
+
+                self_input(R, xin(m))
+
+                @pl.when(m == 1)
+                def _():
+                    all_finish(g, 1)
+                    small_middle()
+                    all_start(g, 2)
+
+                store_x(m).start()
+
+            def store_x(m):
+                return pltpu.make_async_copy(xin(m), tok.at[0, m], osem.at[m])
+
             prefix_setup(R)
+            twice(forward)
+            twice(backward)
+            small_late()
+            all_finish(w.at[12], 2)
+            store_x(0).wait()
+            store_x(1).wait()
+            small_finish()
+
+        def decoder():
+            R = tgt_rows
+
+            def shifted(r):
+                return pl.ds(pl.multiple_of(r.start + R, LN_ROWS), LN_ROWS)
 
             def pick(c):
                 parts = [pw[1, 2 * c + i // 2, pl.ds((i % 2) * R, R), 256:512] for i in range(4)]
@@ -564,7 +626,7 @@
             slope = (pick, put)
 
             def early(m):
-                return f1.at[pl.ds(R, R)] if m == 0 else da
+                return da.at[m]
 
             def dq_(m):
                 return k.at[m, pl.ds(dec_keys, R)]
@@ -580,21 +642,23 @@
 
             def self_forward(m):
                 load_t(m).wait()
-                if m == 0:
+
+                @pl.when(m == 0)
+                def _():
                     for b in range(3):
                         fetch(b).wait()
+
                 project(R, dxin.at[m], dq_(m), m)
                 key = lax.broadcasted_iota(jnp.int32, (dec_keys, PAIR), 0)
                 query = lax.broadcasted_iota(jnp.int32, (dec_keys, PAIR), 1)
                 seen = (key <= query) | ((key >= R) & (key < R + PRE))
                 bias[0:dec_keys] = jnp.where(seen, 0.0, NEG)
                 attend(
-                    R, R, True, pairs, dq_(m), k.at[m, pl.ds(0, dec_keys)],
+                    SELF_PAIRS, R, R, True, pairs, dq_(m), k.at[m, pl.ds(0, dec_keys)],
                     tt.at[:, pl.ds(0, R)], vtp, self_probs(m), bias.at[pl.ds(0, dec_keys)],
                     ot.at[:, pl.ds(0, R)],
                 )
-                if m == 0:
-                    fetch(3).wait()
+                pl.when(m == 0)(fetch(3).wait)
                 f1[0:R] = dxin[m].astype(F32) + dot(ot[:, 0:R].T, w[3])
 
                 def norm(r):
@@ -606,15 +670,18 @@
                     xh1[m, shifted(r)] = h.astype(BF)
 
                 by_rows(R, norm)
-                if m == 0:
-                    fetch(12).wait()
+                pl.when(m == 0)(fetch(12).wait)
                 dqc_(m)[...] = (dot(xh1[m, R : 2 * R], w[12]) * 0.125).astype(BF)
 
             def middle(m):
-                cross_copy(m).wait_recv()
-                if m == 0:
+                for i in range(src_rows // PAIR):
+                    memory_copy(m, i).wait_recv()
+
+                @pl.when(m == 0)
+                def _():
                     fetch(13).wait()
                     fetch(14).wait()
+
                 keys = dot(rcv[m], w[13]).astype(BF)
                 kc[...] = keys
                 kct[...] = keys.T
@@ -624,11 +691,10 @@
                 key = lax.broadcasted_iota(jnp.int32, (src_rows, PAIR), 0)
                 bias[0:src_rows] = jnp.where(key < sl[m], 0.0, NEG)
                 attend(
-                    R, src_rows, False, pairs, dqc_(m), kc, tt, None, cross_probs(),
+                    CROSS_PAIRS, R, src_rows, False, pairs, dqc_(m), kc, tt, None, cross_probs(),
                     bias.at[pl.ds(0, src_rows)], ot.at[:, pl.ds(0, R)],
                 )
-                if m == 0:
-                    fetch(15).wait()
+                pl.when(m == 0)(fetch(15).wait)
                 f1[0:R] = early(m)[...] + dot(ot[:, 0:R].T, w[15])
                 yb = xh1.at[m, pl.ds(R, R)]
 
@@ -641,10 +707,8 @@
                     yb[r] = h.astype(BF)
 
                 by_rows(R, norm)
-                branch(R, yb, slope, m, (lambda b: fetch(b).wait()) if m == 0 else None)
-                if m == 0:
-                    load_c(0).wait()
-                    load_c(1).wait()
+                branch(DEC_CHUNKS, R, yb, slope, m)
+                load_c(m).wait()
                 df = xh2.at[m, pl.ds(R, R)]
 
                 def turn(r):
@@ -660,10 +724,17 @@
                 by_rows(R, turn)
                 store_d(m).start()
                 branch_back_adapter(R, df, m)
-                branch_back_feed(R, df, slope, m)
-                if m == 1:
+                branch_back_feed(DEC_CHUNKS, R, df, slope, m, True)
+
+                @pl.when(m == 1)
+                def _():
+                    for b in range(4):
+                        fetch(b).start()
                     write_grads(
-                        g, xh1[:, R : 2 * R].reshape(2 * R, features), xh2[:, R : 2 * R].reshape(2 * R, features), 2 * R
+                        g,
+                        lambda r: xh1[:, R : 2 * R, r].reshape(2 * R, 2 * PAIR),
+                        lambda: xh2[:, R : 2 * R].reshape(2 * R, features),
+                        2 * R,
                     )
                     all_start(g, 0)
 
@@ -676,14 +747,21 @@
                 grad_mixed = dot_t(dqkv[0, 0:R], w[15]).astype(BF)
                 dqkv[0, 0:R] = grad_mixed
                 attend_back(
-                    R, src_rows, False, pairs, dqkv.at[0, pl.ds(0, R)], dqc_(m), kc, vc, kct, None,
-                    cross_probs(), ot.at[:, pl.ds(0, R)], dqkv.at[1], dqkv.at[2], None,
+                    CROSS_PAIRS, R, src_rows, False, pairs, dqkv.at[0, pl.ds(0, R)], dqc_(m), kc, vc, kct, None,
+                    cross_probs(), kt.at[m, :, pl.ds(R, R)], dqkv.at[1], dqkv.at[2], None,
                 )
-                if m == 1:
-                    cross_copy(0).wait_send()
-                snd[...] = (dot_t(dqkv[1], w[13]) + dot_t(dqkv[2], w[14])).astype(BF)
-                cross_copy(m).start()
-                early(m)[...] = f1[0:R] + dot_t(ot[:, 0:R].T, w[12])
+
+                @pl.when(m == 1)
+                def _():
+                    back_copy(0, 0).wait_send()
+                    back_copy(0, 1).wait_send()
+
+                span = features // 2
+                for i in range(2):
+                    part = pl.ds(i * span, span)
+                    snd[:, part] = (dot_t(dqkv[1], w[13, part]) + dot_t(dqkv[2], w[14, part])).astype(BF)
+                    back_copy(m, i).start()
+                early(m)[...] = f1[0:R]
 
             def store_d(m):
                 return pltpu.make_async_copy(dct.at[m], tok.at[0, m, pl.ds(0, R)], osem.at[m])
@@ -692,32 +770,53 @@
                 return pltpu.make_async_copy(dxin.at[m], tok.at[0, m, pl.ds(R, R)], osem.at[2 + m])
 
             g = w.at[8]
-            self_forward(0)
-            self_forward(1)
-            middle(0)
-            middle(1)
+            prefix_setup(R)
+            twice(self_forward)
+
+            def turn_block(c, carry):
+                fetch_in(c).wait()
+                w[c] = w[4 + c].T
+                return carry
+
+            lax.fori_loop(0, chunks, turn_block, 0)
+            twice(middle)
             all_finish(g, 0)
             all_start(g, 1)
-            for m in range(2):
-                f1[0:R] = early(m)[...]
-                self_back(R, m, dq_(m))
-                if m == 0:
-                    self_input(R, dxin.at[m])
-                    store_y(m).start()
+            for b in range(4):
+                fetch(b).wait()
+
+            def last(m):
+                f1[0:R] = early(m)[...] + dot_t(kt[m, :, R : 2 * R].T, w[12])
+                self_back(SELF_PAIRS, R, m, dq_(m))
+                pl.when(m == 1)(small_begin)
+                self_input(R, dxin.at[m])
+                store_y(m).start()
+
+                @pl.when(m == 0)
+                def _():
                     all_finish(g, 1)
                     all_start(g, 2)
-            small_begin()
-            self_input(R, dxin.at[1])
-            store_y(1).start()
+
+            twice(last)
             small_middle()
             all_finish(g, 2)
             small_late()
             for m in range(2):
                 store_d(m).wait()
                 store_y(m).wait()
-            cross_copy(1).wait_send()
+            back_copy(1, 0).wait_send()
+            back_copy(1, 1).wait_send()
             small_finish()
 
+        @pl.when(section == 0)
+        def _():
+            encoder_loads()
+
+        @pl.when(section == 1)
+        def _():
+            decoder_loads()
+
+        greet()
         pl.when(section == 0)(encoder)
         pl.when(section == 1)(decoder)
 
@@ -766,15 +865,15 @@
         vm((small_rows, features), BF),
         vm((2, tgt_rows, features), BF),
         vm((2, tgt_rows, features), BF),
-        vm((tgt_rows, features), F32),
+        vm((2, tgt_rows, features), F32),
         vm((src_rows, features), BF),
         vm((src_rows, features), BF),
         vm((features, src_rows), BF),
         pltpu.SemaphoreType.DMA((18,)),
         pltpu.SemaphoreType.DMA((4,)),
         pltpu.SemaphoreType.DMA((4,)),
-        pltpu.SemaphoreType.DMA((2,)),
-        pltpu.SemaphoreType.DMA((2,)),
+        pltpu.SemaphoreType.DMA((4,)),
+        pltpu.SemaphoreType.DMA((4,)),
         pltpu.SemaphoreType.DMA((18,)),
         pltpu.SemaphoreType.DMA((18,)),
         pltpu.SemaphoreType.DMA((smalls,)),

time: 133 us -> 101 us (0.76)
  Pallas kernels: 133 us -> 100 us
    pallas_call x1, Pallas kernels: 130 us -> 96.8 us  [per_device(): pl.pallas_call(kernel, out_shape=(jax.ShapeDtypeStruct((1, source.shape[0...]
where the time goes in v1:
time: 101 us
  Pallas kernels  100 us (99%)
    pallas_call x1, Pallas kernels, per_device(): pl.pallas_call(kernel, out_shape=(jax.ShapeDtypeStruct((1, source.shape[0...  96.8 us
    pallas_call x1, Pallas kernels, per_device(): pl.pallas_call(finish, out_shape=(jax.ShapeDtypeStruct(tok.shape, BF), ja...  3.45 us

profile of v1, /device:TPU:0, one launch (start us, length us, event | category | flops | bytes accessed | tf_op | source)
XLA Modules:
  0.0 101.1 jit_solution(11519047641210763674)
XLA Ops:
  0.6 96.8 %shard_map.217 = (bf16[1,2,256,1024]{3,2,1,0:T(8,128)(2,1)}, f32[64,512]{1,0:T(8,128)}, f32[32,1024]{1,0:T(8,128)}, f32[64,1024]{1,0:T(8,128)}) custom-call(bf16[2,256,1024]{2,1,0:T(8,128)(2,1)} %src.1, bf16[2,128,1024]{2,1,0:T(8,128)(2,1)} %tgt.1, bf16[2,128,1024]{2,1,0:T(8,128)(2,1)} %ct.1, s32[2]{0:T(128)} %bitcast.9, s32[2]{0:T(128)} %bitcast.10, ...), custom_call_target="tpu_custom_call" | custom-call | tf_op jit(solution)/shard_map/pallas_call | solution.py:917
  97.5 3.4 %shard_map.218 = (bf16[1,2,256,1024]{3,2,1,0:T(8,128)(2,1)}, f32[30,2,1024]{2,1,0:T(2,128)}, f32[1,64,512]{2,1,0:T(8,128)}, f32[1,32,1024]{2,1,0:T(8,128)}, f32[1,512]{1,0:T(1,128)}, /*index=5*/f32[1,1024]{1,0:T(1,128)}) custom-call(bf16[1,2,256,1024]{3,2,1,0:T(8,128)(2,1)} %get-tuple-element.16.tok, f32[64,512]{1,0:T(8,128)} %get-tuple-element.17.ig, ...), custom_call_target="tpu_custom_call" | custom-call | tf_op jit(solution)/shard_map/pallas_call | solution.py:936

commit v2 on v1

--- a/solution.py
+++ b/solution.py
@@ -19,11 +19,13 @@
 PAIR = 128
 HALF = 64
 LN_ROWS = 128
-ENC_PAIRS = 4
+ENC_PAIRS = 8
 SELF_PAIRS = 2
 CROSS_PAIRS = 8
 ENC_CHUNKS = 1
 DEC_CHUNKS = 4
+ENC_GRADS = 1
+DEC_GRADS = 4
 
 
 def dot(a, b):
@@ -214,18 +216,22 @@
                 return pl.multiple_of(((x * ny + y) * nz + z) * ra, ra)
             return pl.multiple_of(((y * nx + x) * nz + z) * ra, ra)
 
-        def write_grads(g, ybs, dfs, count):
+        def write_in(unroll, g, ybs, count):
             group = 2 * PAIR
-            half = ra // 2
-
-            def first(t, carry):
+
+            def step(t, carry):
                 block = tdot(ybs(rows_of(t * group, group)), dz[0:count])
                 for i in range(group // ra):
                     d = t * (group // ra) + i
                     g[pl.ds(place(d, "A"), ra), 0:adapt] = block[i * ra : (i + 1) * ra].astype(BF)
                 return carry
 
-            def second(t, carry):
+            lax.fori_loop(0, features // group, step, 0, unroll=unroll)
+
+        def write_out(unroll, g, dfs, count):
+            half = ra // 2
+
+            def step(t, carry):
                 block = 4.0 * tdot(rb[0:count, rows_of(t * PAIR, PAIR)], dfs())
                 for i in range(PAIR // half):
                     d = t * (PAIR // half) + i
@@ -234,27 +240,29 @@
                     g[pl.ds(place(d, "B"), ra), adapt : 2 * adapt] = part.astype(BF)
                 return carry
 
-            lax.fori_loop(0, features // group, first, 0)
-            lax.fori_loop(0, adapt // PAIR, second, 0)
-
-        def all_start(g, stage):
-            for part in "AB":
-                for c in reduce_phase(part, stage, g):
-                    c.start()
-
-        def all_finish(g, stage):
-            for part in "AB":
-                for c in reduce_phase(part, stage, g):
-                    c.wait()
-                total = reduce_sum(part, stage, g)
-                if stage < 2:
-                    landing[part][stage][0] = total.astype(BF)
-                elif part == "A":
-                    ig_out[...] = total
-                else:
-                    half = ra // 2
-                    og_out[:, 0:adapt] = total[:half]
-                    og_out[:, adapt : 2 * adapt] = total[half:]
+            lax.fori_loop(0, adapt // PAIR, step, 0, unroll=unroll)
+
+        def start(part, stage, g):
+            for c in reduce_phase(part, stage, g):
+                c.start()
+
+        def finish_stage(part, stage, g):
+            for c in reduce_phase(part, stage, g):
+                c.wait()
+            total = reduce_sum(part, stage, g)
+            if stage < 2:
+                landing[part][stage][0] = total.astype(BF)
+                start(part, stage + 1, g)
+            elif part == "A":
+                ig_out[...] = total
+            else:
+                half = ra // 2
+                og_out[:, 0:adapt] = total[:half]
+                og_out[:, adapt : 2 * adapt] = total[half:]
+
+        def finish_both(stage, g):
+            finish_stage("B", stage, g)
+            finish_stage("A", stage, g)
 
         plane = nx * ny
         piece = small_rows * features // (16 * plane)
@@ -377,11 +385,6 @@
             tt[:, 0:rows] = values.T
 
         def branch(unroll, rows, yb, slope, m):
-            @pl.when(m == 0)
-            def _():
-                fetch(16).wait()
-                fetch(17).wait()
-
             pre = dot(yb[...], wdi[...]) + bi[...].astype(F32)
             act, turn = gelu_and_slope(pre)
             act = act.astype(BF)
@@ -389,13 +392,14 @@
             sa[m, 0:rows] = turn.astype(BF)
             f1[0:rows] = f1[0:rows] + 4.0 * (dot(act, wdo[...]) + bo[...].astype(F32))
 
-            def step(c, carry):
+            if rows == src_rows:
+
                 @pl.when(m == 0)
                 def _():
-                    if rows == src_rows:
-                        fetch_in(c).wait()
-                    fetch_out(c).wait()
-
+                    for b in (4, 8, 5, 9, 6, 10, 7, 11):
+                        fetch(b).wait()
+
+            def step(c, carry):
                 act, turn = gelu_and_slope(dot(yb[...], w[4 + c]))
                 slope[1](c, turn.astype(BF))
                 f1[0:rows] = f1[0:rows] + dot(act.astype(BF), w[8 + c])
@@ -477,10 +481,6 @@
             for b in [0, 1, 2]:
                 fetch(b).start()
             load_t(1).start()
-            for b in [3, 12, 13, 14, 15, 16, 17, 4, 8, 5, 9, 6, 10, 7, 11]:
-                fetch(b).start()
-            load_c(0).start()
-            load_c(1).start()
 
         def encoder():
             R = src_rows
@@ -520,7 +520,12 @@
                 attend(
                     ENC_PAIRS, R, R, True, pairs, q(m), k.at[m], tt, vtp, lambda p: pw.at[m, p], bias, ot,
                 )
-                pl.when(m == 0)(fetch(3).wait)
+
+                @pl.when(m == 0)
+                def _():
+                    for b in (3, 16, 17):
+                        fetch(b).wait()
+
                 f1[...] = xin(m)[...].astype(F32) + dot(ot[...].T, w[3])
 
                 def norm(r):
@@ -565,35 +570,40 @@
                     df(m)[r] = dt.astype(BF)
 
                 by_rows(R, norm)
-                branch_back_adapter(R, df(m), m)
                 g = w.at[12]
 
                 @pl.when(m == 1)
                 def _():
-                    write_grads(g, lambda r: w[14, 0 : 2 * R, r], lambda: w[14, 512 : 512 + 2 * R], 2 * R)
-                    all_start(g, 0)
+                    write_out(ENC_GRADS, g, lambda: w[14, 512 : 512 + 2 * R], 2 * R)
+                    start("B", 0, g)
+
+                branch_back_adapter(R, df(m), m)
+
+                @pl.when(m == 1)
+                def _():
+                    write_in(ENC_GRADS, g, lambda r: w[14, 0 : 2 * R, r], 2 * R)
+                    start("A", 0, g)
 
                 branch_back_feed(ENC_CHUNKS, R, df(m), slope(m), m, False)
 
                 def between():
                     @pl.when(m == 1)
                     def _():
-                        all_finish(g, 0)
-                        all_start(g, 1)
+                        finish_both(0, g)
 
                 self_back(ENC_PAIRS, R, m, q(m), between)
 
                 @pl.when(m == 1)
                 def _():
                     small_begin()
+                    finish_stage("B", 1, g)
 
                 self_input(R, xin(m))
 
                 @pl.when(m == 1)
                 def _():
-                    all_finish(g, 1)
                     small_middle()
-                    all_start(g, 2)
+                    finish_stage("A", 1, g)
 
                 store_x(m).start()
 
@@ -604,7 +614,7 @@
             twice(forward)
             twice(backward)
             small_late()
-            all_finish(w.at[12], 2)
+            finish_both(2, w.at[12])
             store_x(0).wait()
             store_x(1).wait()
             small_finish()
@@ -612,9 +622,6 @@
         def decoder():
             R = tgt_rows
 
-            def shifted(r):
-                return pl.ds(pl.multiple_of(r.start + R, LN_ROWS), LN_ROWS)
-
             def pick(c):
                 parts = [pw[1, 2 * c + i // 2, pl.ds((i % 2) * R, R), 256:512] for i in range(4)]
                 return jnp.concatenate(parts, axis=1)
@@ -625,9 +632,6 @@
 
             slope = (pick, put)
 
-            def early(m):
-                return da.at[m]
-
             def dq_(m):
                 return k.at[m, pl.ds(dec_keys, R)]
 
@@ -640,47 +644,106 @@
             def cross_probs():
                 return lambda p: pw.at[0, p, pl.ds(0, src_rows), pl.ds(2 * R, 2 * R)]
 
-            def self_forward(m):
-                load_t(m).wait()
-
-                @pl.when(m == 0)
-                def _():
-                    for b in range(3):
-                        fetch(b).wait()
-
-                project(R, dxin.at[m], dq_(m), m)
+            def self_forward():
+                load_t(0).wait()
+                load_t(1).wait()
+                fetch(0).wait()
+                for b in (3, 12, 4, 5, 6, 7):
+                    fetch(b).start()
+                rows = dxin[...].reshape(2 * R, features)
+                queries = (dot(rows, w[0]) * 0.125).astype(BF)
+                fetch(1).wait()
+                keys = dot(rows, w[1]).astype(BF)
+                fetch(2).wait()
+                for b in (13, 14, 15, 16, 17, 8, 9, 10, 11):
+                    fetch(b).start()
+                load_c(0).start()
+                load_c(1).start()
+                values = dot(rows, w[2]).astype(BF)
+                for m in range(2):
+                    own = slice(m * R, (m + 1) * R)
+                    dq_(m)[...] = queries[own]
+                    k[m, 0:R] = keys[own]
+                    kt[m, :, 0:R] = keys[own].T
+                    v[m, 0:R] = values[own]
+                tt[...] = values.T
                 key = lax.broadcasted_iota(jnp.int32, (dec_keys, PAIR), 0)
                 query = lax.broadcasted_iota(jnp.int32, (dec_keys, PAIR), 1)
                 seen = (key <= query) | ((key >= R) & (key < R + PRE))
                 bias[0:dec_keys] = jnp.where(seen, 0.0, NEG)
-                attend(
-                    SELF_PAIRS, R, R, True, pairs, dq_(m), k.at[m, pl.ds(0, dec_keys)],
-                    tt.at[:, pl.ds(0, R)], vtp, self_probs(m), bias.at[pl.ds(0, dec_keys)],
-                    ot.at[:, pl.ds(0, R)],
-                )
-                pl.when(m == 0)(fetch(3).wait)
-                f1[0:R] = dxin[m].astype(F32) + dot(ot[:, 0:R].T, w[3])
-
-                def norm(r):
-                    shaped, factor = norm_of(f1[r])
-                    xh1[m, r] = shaped.astype(BF)
-                    r1[m, r] = factor
+
+                def mix(m):
+                    attend(
+                        SELF_PAIRS, R, R, True, pairs, dq_(m), k.at[m, pl.ds(0, dec_keys)],
+                        tt.at[:, rows_of(m * R, R)], vtp, self_probs(m), bias.at[pl.ds(0, dec_keys)],
+                        ot.at[:, rows_of(m * R, R)],
+                    )
+
+                twice(mix)
+                fetch(3).wait()
+                f1[...] = dxin[...].reshape(2 * R, features).astype(F32) + dot(ot[...].T, w[3])
+
+                def norm(m):
+                    shaped, factor = norm_of(f1[rows_of(m * R, R)])
+                    xh1[m, 0:R] = shaped.astype(BF)
+                    r1[m, 0:R] = factor
                     h = shaped * gain(0)
-                    early(m)[r] = h
-                    xh1[m, shifted(r)] = h.astype(BF)
-
-                by_rows(R, norm)
-                pl.when(m == 0)(fetch(12).wait)
-                dqc_(m)[...] = (dot(xh1[m, R : 2 * R], w[12]) * 0.125).astype(BF)
+                    da[m] = h
+                    xh1[m, R : 2 * R] = h.astype(BF)
+
+                twice(norm)
+                fetch(12).wait()
+                crossed = (dot(xh1[:, R : 2 * R].reshape(2 * R, features), w[12]) * 0.125).astype(BF)
+                for m in range(2):
+                    dqc_(m)[...] = crossed[m * R : (m + 1) * R]
+
+            def self_backward(g):
+                sides = jnp.concatenate([kt[m, :, R : 2 * R].T for m in range(2)], axis=0)
+                f1[...] = da[...].reshape(2 * R, features) + dot_t(sides, w[12])
+
+                def norm(m):
+                    r = rows_of(m * R, R)
+                    dt = norm_back(f1[r], xh1[m, 0:R].astype(F32), r1[m, 0:R], gain(0))
+                    f1[r] = dt
+                    dqkv[0, r] = dt.astype(BF)
+
+                for b in range(4):
+                    fetch(b).wait()
+                twice(norm)
+                dqkv[0] = dot_t(dqkv[0], w[3]).astype(BF)
+                finish_both(0, g)
+
+                def unmix(m):
+                    r = rows_of(m * R, R)
+                    attend_back(
+                        SELF_PAIRS, R, R, True, pairs, dqkv.at[0, r], dq_(m),
+                        k.at[m, pl.ds(0, dec_keys)], v.at[m, pl.ds(0, dec_keys)],
+                        kt.at[m, :, pl.ds(0, R)], ktp, self_probs(m),
+                        ot.at[:, r], dqkv.at[1, r], dqkv.at[2, r], pre_sum,
+                    )
+
+                twice(unmix)
+                dqkv[0] = ot[...].T
+                small_begin()
+                finish_both(1, g)
+                total = f1[...]
+                for b in range(3):
+                    total = total + dot_t(dqkv[b], w[b])
+                low = total.astype(BF)
+                for m in range(2):
+                    dxin[m] = low[m * R : (m + 1) * R]
+                    store_y(m).start()
 
             def middle(m):
+                @pl.when(m == 0)
+                def _():
+                    for b in (13, 14, 15, 16, 17, 8, 9, 10, 11):
+                        fetch(b).wait()
+                    load_c(0).wait()
+                    load_c(1).wait()
+
                 for i in range(src_rows // PAIR):
                     memory_copy(m, i).wait_recv()
-
-                @pl.when(m == 0)
-                def _():
-                    fetch(13).wait()
-                    fetch(14).wait()
 
                 keys = dot(rcv[m], w[13]).astype(BF)
                 kc[...] = keys
@@ -694,8 +757,7 @@
                     CROSS_PAIRS, R, src_rows, False, pairs, dqc_(m), kc, tt, None, cross_probs(),
                     bias.at[pl.ds(0, src_rows)], ot.at[:, pl.ds(0, R)],
                 )
-                pl.when(m == 0)(fetch(15).wait)
-                f1[0:R] = early(m)[...] + dot(ot[:, 0:R].T, w[15])
+                f1[0:R] = da[m] + dot(ot[:, 0:R].T, w[15])
                 yb = xh1.at[m, pl.ds(R, R)]
 
                 def norm(r):
@@ -708,7 +770,6 @@
 
                 by_rows(R, norm)
                 branch(DEC_CHUNKS, R, yb, slope, m)
-                load_c(m).wait()
                 df = xh2.at[m, pl.ds(R, R)]
 
                 def turn(r):
@@ -728,15 +789,14 @@
 
                 @pl.when(m == 1)
                 def _():
+                    back_copy(0, 0).wait_send()
+                    back_copy(0, 1).wait_send()
                     for b in range(4):
                         fetch(b).start()
-                    write_grads(
-                        g,
-                        lambda r: xh1[:, R : 2 * R, r].reshape(2 * R, 2 * PAIR),
-                        lambda: xh2[:, R : 2 * R].reshape(2 * R, features),
-                        2 * R,
-                    )
-                    all_start(g, 0)
+                    write_out(DEC_GRADS, g, lambda: xh2[:, R : 2 * R].reshape(2 * R, features), 2 * R)
+                    start("B", 0, g)
+                    write_in(DEC_GRADS, g, lambda r: xh1[:, R : 2 * R, r].reshape(2 * R, 2 * PAIR), 2 * R)
+                    start("A", 0, g)
 
                 def back(r):
                     dt = norm_back(f1[r], xh2[m, r].astype(F32), r2[m, r], gain(1))
@@ -751,17 +811,12 @@
                     cross_probs(), kt.at[m, :, pl.ds(R, R)], dqkv.at[1], dqkv.at[2], None,
                 )
 
-                @pl.when(m == 1)
-                def _():
-                    back_copy(0, 0).wait_send()
-                    back_copy(0, 1).wait_send()
-
                 span = features // 2
                 for i in range(2):
                     part = pl.ds(i * span, span)
                     snd[:, part] = (dot_t(dqkv[1], w[13, part]) + dot_t(dqkv[2], w[14, part])).astype(BF)
                     back_copy(m, i).start()
-                early(m)[...] = f1[0:R]
+                da[m] = f1[0:R]
 
             def store_d(m):
                 return pltpu.make_async_copy(dct.at[m], tok.at[0, m, pl.ds(0, R)], osem.at[m])
@@ -771,7 +826,7 @@
 
             g = w.at[8]
             prefix_setup(R)
-            twice(self_forward)
+            self_forward()
 
             def turn_block(c, carry):
                 fetch_in(c).wait()
@@ -780,26 +835,9 @@
 
             lax.fori_loop(0, chunks, turn_block, 0)
             twice(middle)
-            all_finish(g, 0)
-            all_start(g, 1)
-            for b in range(4):
-                fetch(b).wait()
-
-            def last(m):
-                f1[0:R] = early(m)[...] + dot_t(kt[m, :, R : 2 * R].T, w[12])
-                self_back(SELF_PAIRS, R, m, dq_(m))
-                pl.when(m == 1)(small_begin)
-                self_input(R, dxin.at[m])
-                store_y(m).start()
-
-                @pl.when(m == 0)
-                def _():
-                    all_finish(g, 1)
-                    all_start(g, 2)
-
-            twice(last)
+            self_backward(g)
             small_middle()
-            all_finish(g, 2)
+            finish_both(2, g)
             small_late()
             for m in range(2):
                 store_d(m).wait()
@@ -882,9 +920,19 @@
     return kernel, scratch, ra
 
 
-def finish(tok, ig, og, small, tok_out, pre_out, ig_out, og_out, ib_out, ob_out, sem):
-    copy = pltpu.make_async_copy(tok, tok_out, sem)
-    copy.start()
+def finish(tok, ig_in, og_in, small_in, tok_out, pre_out, ig_out, og_out, ib_out, ob_out, held, ig, og, small, sem):
+    micro = tok.shape[1]
+    loads = [pltpu.make_async_copy(tok.at[0, m], held.at[0, m], sem.at[m]) for m in range(micro)]
+    stores = [pltpu.make_async_copy(held.at[0, m], tok_out.at[0, m], sem.at[micro + m]) for m in range(micro)]
+    rest = [(small_in, small, 4), (ig_in, ig, 5), (og_in, og, 6)]
+    rest = [pltpu.make_async_copy(a, b, sem.at[i]) for a, b, i in rest]
+    for copy in loads + rest:
+        copy.start()
+    for load, store in zip(loads, stores):
+        load.wait()
+        store.start()
+    for copy in rest:
+        copy.wait()
     adapt = ig.shape[1]
     pre_out[:, 0, :] = small[0:PRE]
     pre_out[:, 1, :] = small[PRE_PAD : PRE_PAD + PRE]
@@ -892,7 +940,8 @@
     og_out[0] = og[...]
     ob_out[...] = small[PRE : PRE + 1]
     ib_out[...] = small[PRE_PAD + PRE : PRE_PAD + PRE + 1, 0:adapt]
-    copy.wait()
+    for store in stores:
+        store.wait()
 
 
 def solution(mesh):
@@ -943,9 +992,15 @@
                 jax.ShapeDtypeStruct((1, adapt), F32),
                 jax.ShapeDtypeStruct((1, features), F32),
             ),
-            in_specs=[anywhere, vector, vector, vector],
-            out_specs=(vector, vector, vector, vector, vector, vector),
-            scratch_shapes=[pltpu.SemaphoreType.DMA(())],
+            in_specs=[anywhere, anywhere, anywhere, anywhere],
+            out_specs=(anywhere, vector, vector, vector, vector, vector),
+            scratch_shapes=[
+                pltpu.VMEM(tok.shape, BF),
+                pltpu.VMEM(ig.shape, F32),
+                pltpu.VMEM(og.shape, F32),
+                pltpu.VMEM(small.shape, F32),
+                pltpu.SemaphoreType.DMA((7,)),
+            ],
         )(tok, ig, og, small)
         return tok, pre.transpose(1, 0, 2)[None], ig, og, ib, ob
 

time: 101 us -> 95.9 us (0.950)
  Pallas kernels: 100 us -> 94.8 us
    pallas_call x1, Pallas kernels: 96.8 us -> 92 us  [per_device(): pl.pallas_call(kernel, out_shape=(jax.ShapeDtypeStruct((1, source.shape[0...]
where the time goes in v2:
time: 95.9 us; the launch traced here: 95.7 us
  Pallas kernels  94.8 us (99%)
    pallas_call x1, Pallas kernels, per_device(): pl.pallas_call(kernel, out_shape=(jax.ShapeDtypeStruct((1, source.shape[0...  92 us
    pallas_call x1, Pallas kernels, per_device(): pl.pallas_call(finish, out_shape=(jax.ShapeDtypeStruct(tok.shape, BF), ja...  2.85 us

profile of v2, /device:TPU:0, one launch (start us, length us, event | category | flops | bytes accessed | tf_op | source)
XLA Modules:
  0.0 95.7 jit_solution(6901451575895735589)
XLA Ops:
  0.6 92.0 %shard_map.217 = (bf16[1,2,256,1024]{3,2,1,0:T(8,128)(2,1)}, f32[64,512]{1,0:T(8,128)}, f32[32,1024]{1,0:T(8,128)}, f32[64,1024]{1,0:T(8,128)}) custom-call(bf16[2,256,1024]{2,1,0:T(8,128)(2,1)} %src.1, bf16[2,128,1024]{2,1,0:T(8,128)(2,1)} %tgt.1, bf16[2,128,1024]{2,1,0:T(8,128)(2,1)} %ct.1, s32[2]{0:T(128)} %bitcast.9, s32[2]{0:T(128)} %bitcast.10, ...), custom_call_target="tpu_custom_call" | custom-call | tf_op jit(solution)/shard_map/pallas_call | solution.py:966
  92.6 2.9 %shard_map.218 = (bf16[1,2,256,1024]{3,2,1,0:T(8,128)(2,1)}, f32[30,2,1024]{2,1,0:T(2,128)}, f32[1,64,512]{2,1,0:T(8,128)}, f32[1,32,1024]{2,1,0:T(8,128)}, f32[1,512]{1,0:T(1,128)}, /*index=5*/f32[1,1024]{1,0:T(1,128)}) custom-call(bf16[1,2,256,1024]{3,2,1,0:T(8,128)(2,1)} %get-tuple-element.16.tok, f32[64,512]{1,0:T(8,128)} %get-tuple-element.17.ig_in, ...), custom_call_target="tpu_custom_call" | custom-call | tf_op jit(solution)/shard_map/pallas_call | solution.py:985

commit v3 on v2

--- a/solution.py
+++ b/solution.py
@@ -24,6 +24,7 @@
 CROSS_PAIRS = 8
 ENC_CHUNKS = 1
 DEC_CHUNKS = 4
+TURNED = 1
 ENC_GRADS = 1
 DEC_GRADS = 4
 
@@ -96,7 +97,7 @@
     lax.fori_loop(0, pairs, step, 0, unroll=unroll)
 
 
-def attend_back(unroll, rows, tokens, prefixed, pairs, grad, q, k, v, kt, ktp, probs, dq_t, dk, dv, pre_sum):
+def attend_back(unroll, rows, tokens, prefixed, pairs, grad, q, v, kt, ktp, probs, dq_t, dk, dv, pre_sum):
     def step(p, carry):
         lanes = rows_of(p * PAIR, PAIR)
         grads = both_heads(grad[:, lanes])
@@ -137,10 +138,10 @@
     def kernel(
         src, tgt, ct, sl, tl, ai, ao, cq, cp, co, fi, fo, di, do, bi, bo, prefix, gains,
         tok, ig_out, og_out, sm_out,
-        w, wdi, wdo, pw, k, v, kt, tt, ot, ktp, vtp, xh1, xh2, r1, r2, sa, rb, dz, snd, rcv,
+        w, wdi, wdo, pw, k, v, kt, tt, ot, ktp, vtp, xh1, xh2, rr, sa, rb, dz, snd, rcv,
         f1, dqkv, rsx, rsy, rsz, rsa, rsb, rsc, pre_sum, bias, ib_sum, ob_sum,
         small, small_in, small_mid, small_z, small_end, small_all,
-        dxin, dct, da, kc, vc, kct,
+        dxin, dct, da, vc, kct,
         wsem, xsem, osem, ssem, rsem, gss, grs, mss, mrs,
     ):
         section = lax.axis_index("section")
@@ -418,16 +419,24 @@
             f1[0:rows] = f1[0:rows] + dot_t(dz[rows_of(m * rows, rows)], wdi[...])
 
             def step(c, carry):
-                grad = (dot_t(df[...], w[8 + c]) * slope[0](c).astype(F32)).astype(BF)
+                if turned and c < TURNED:
+                    grad = dot(df[...], w[16 + c])
+                else:
+                    grad = dot_t(df[...], w[8 + c])
+                grad = (grad * slope[0](c).astype(F32)).astype(BF)
                 back = dot(grad, w[c]) if turned else dot_t(grad, w[4 + c])
                 f1[0:rows] = f1[0:rows] + back
                 return carry
 
-            lax.fori_loop(0, chunks, step, 0, unroll=unroll)
+            if turned:
+                for c in range(chunks):
+                    step(c, 0)
+            else:
+                lax.fori_loop(0, chunks, step, 0, unroll=unroll)
 
         def self_back(unroll, rows, m, q, between=None):
             def norm(r):
-                dt = norm_back(f1[r], xh1[m, r].astype(F32), r1[m, r], gain(0))
+                dt = norm_back(f1[r], xh1[m, r].astype(F32), rr[m, r, 0:1], gain(0))
                 f1[r] = dt
                 dqkv[0, r] = dt.astype(BF)
 
@@ -438,7 +447,7 @@
                 between()
             attend_back(
                 unroll, rows, rows, True, pairs, dqkv.at[0, pl.ds(0, rows)], q,
-                k.at[m, pl.ds(0, rows + PRE_PAD)], v.at[m, pl.ds(0, rows + PRE_PAD)],
+                v.at[m, pl.ds(0, rows + PRE_PAD)],
                 kt.at[m, :, pl.ds(0, rows)], ktp,
                 lambda p: pw.at[m, p, pl.ds(0, rows + PRE_PAD), pl.ds(0, 2 * rows)],
                 ot.at[:, pl.ds(0, rows)], dqkv.at[1, pl.ds(0, rows)], dqkv.at[2, pl.ds(0, rows)], pre_sum,
@@ -531,7 +540,7 @@
                 def norm(r):
                     shaped, factor = norm_of(f1[r])
                     xh1[m, r] = shaped.astype(BF)
-                    r1[m, r] = factor
+                    rr[m, r, 0:1] = factor
                     h = shaped * gain(0)
                     f1[r] = h
                     yb(m)[r] = h.astype(BF)
@@ -548,7 +557,7 @@
                 def last(r):
                     shaped, factor = norm_of(f1[r])
                     xh2[m, r] = shaped.astype(BF)
-                    r2[m, r] = factor
+                    rr[m, r, 1:2] = factor
                     snd[r] = (shaped * gain(1)).astype(BF)
                     memory_copy(m, r.start // PAIR).start()
 
@@ -565,7 +574,7 @@
                 back_copy(m, 1).wait_recv()
 
                 def norm(r):
-                    dt = norm_back(rcv[m, r].astype(F32), xh2[m, r].astype(F32), r2[m, r], gain(1))
+                    dt = norm_back(rcv[m, r].astype(F32), xh2[m, r].astype(F32), rr[m, r, 1:2], gain(1))
                     f1[r] = dt
                     df(m)[r] = dt.astype(BF)
 
@@ -686,7 +695,7 @@
                 def norm(m):
                     shaped, factor = norm_of(f1[rows_of(m * R, R)])
                     xh1[m, 0:R] = shaped.astype(BF)
-                    r1[m, 0:R] = factor
+                    rr[m, 0:R, 0:1] = factor
                     h = shaped * gain(0)
                     da[m] = h
                     xh1[m, R : 2 * R] = h.astype(BF)
@@ -703,7 +712,7 @@
 
                 def norm(m):
                     r = rows_of(m * R, R)
-                    dt = norm_back(f1[r], xh1[m, 0:R].astype(F32), r1[m, 0:R], gain(0))
+                    dt = norm_back(f1[r], xh1[m, 0:R].astype(F32), rr[m, 0:R, 0:1], gain(0))
                     f1[r] = dt
                     dqkv[0, r] = dt.astype(BF)
 
@@ -717,7 +726,7 @@
                     r = rows_of(m * R, R)
                     attend_back(
                         SELF_PAIRS, R, R, True, pairs, dqkv.at[0, r], dq_(m),
-                        k.at[m, pl.ds(0, dec_keys)], v.at[m, pl.ds(0, dec_keys)],
+                        v.at[m, pl.ds(0, dec_keys)],
                         kt.at[m, :, pl.ds(0, R)], ktp, self_probs(m),
                         ot.at[:, r], dqkv.at[1, r], dqkv.at[2, r], pre_sum,
                     )
@@ -737,7 +746,7 @@
             def middle(m):
                 @pl.when(m == 0)
                 def _():
-                    for b in (13, 14, 15, 16, 17, 8, 9, 10, 11):
+                    for b in (13, 14, 15, 16, 17, *range(8 + TURNED, 8 + chunks)):
                         fetch(b).wait()
                     load_c(0).wait()
                     load_c(1).wait()
@@ -746,7 +755,7 @@
                     memory_copy(m, i).wait_recv()
 
                 keys = dot(rcv[m], w[13]).astype(BF)
-                kc[...] = keys
+                dqkv[1] = keys
                 kct[...] = keys.T
                 values = dot(rcv[m], w[14]).astype(BF)
                 vc[...] = values
@@ -754,7 +763,7 @@
                 key = lax.broadcasted_iota(jnp.int32, (src_rows, PAIR), 0)
                 bias[0:src_rows] = jnp.where(key < sl[m], 0.0, NEG)
                 attend(
-                    CROSS_PAIRS, R, src_rows, False, pairs, dqc_(m), kc, tt, None, cross_probs(),
+                    CROSS_PAIRS, R, src_rows, False, pairs, dqc_(m), dqkv.at[1], tt, None, cross_probs(),
                     bias.at[pl.ds(0, src_rows)], ot.at[:, pl.ds(0, R)],
                 )
                 f1[0:R] = da[m] + dot(ot[:, 0:R].T, w[15])
@@ -763,7 +772,7 @@
                 def norm(r):
                     shaped, factor = norm_of(f1[r])
                     xh2[m, r] = shaped.astype(BF)
-                    r2[m, r] = factor
+                    rr[m, r, 1:2] = factor
                     h = shaped * gain(1)
                     f1[r] = h
                     yb[r] = h.astype(BF)
@@ -799,7 +808,7 @@
                     start("A", 0, g)
 
                 def back(r):
-                    dt = norm_back(f1[r], xh2[m, r].astype(F32), r2[m, r], gain(1))
+                    dt = norm_back(f1[r], xh2[m, r].astype(F32), rr[m, r, 1:2], gain(1))
                     f1[r] = dt
                     dqkv[0, r] = dt.astype(BF)
 
@@ -807,7 +816,7 @@
                 grad_mixed = dot_t(dqkv[0, 0:R], w[15]).astype(BF)
                 dqkv[0, 0:R] = grad_mixed
                 attend_back(
-                    CROSS_PAIRS, R, src_rows, False, pairs, dqkv.at[0, pl.ds(0, R)], dqc_(m), kc, vc, kct, None,
+                    CROSS_PAIRS, R, src_rows, False, pairs, dqkv.at[0, pl.ds(0, R)], dqc_(m), vc, kct, None,
                     cross_probs(), kt.at[m, :, pl.ds(R, R)], dqkv.at[1], dqkv.at[2], None,
                 )
 
@@ -834,6 +843,9 @@
                 return carry
 
             lax.fori_loop(0, chunks, turn_block, 0)
+            for c in range(TURNED):
+                fetch_out(c).wait()
+                w[16 + c] = w[8 + c].T
             twice(middle)
             self_backward(g)
             small_middle()
@@ -863,7 +875,7 @@
     piece = small_rows * features // (16 * plane)
     smalls = 2 * (plane - 1) + nz - 1
     scratch = [
-        vm((16, features, features), BF),
+        vm((16 + TURNED, features, features), BF),
         vm((features, adapt), BF),
         vm((adapt, features), BF),
         vm((2, pairs, enc_keys, 2 * src_rows), BF),
@@ -876,8 +888,7 @@
         vm((features, PRE_PAD), BF),
         vm((2, src_rows, features), BF),
         vm((2, src_rows, features), BF),
-        vm((2, src_rows, 1), F32),
-        vm((2, src_rows, 1), F32),
+        vm((2, src_rows, 2), F32),
         vm((2, src_rows, adapt), BF),
         vm((2 * src_rows, adapt), BF),
         vm((2 * src_rows, adapt), BF),
@@ -904,7 +915,6 @@
         vm((2, tgt_rows, features), BF),
         vm((2, tgt_rows, features), BF),
         vm((2, tgt_rows, features), F32),
-        vm((src_rows, features), BF),
         vm((src_rows, features), BF),
         vm((features, src_rows), BF),
         pltpu.SemaphoreType.DMA((18,)),

time: 95.9 us -> 95.2 us (level)
  no operation moved by 1% of the time
where the time goes in v3:
time: 95.2 us; the launch traced here: 95 us
  Pallas kernels  94.1 us (99%)
    pallas_call x1, Pallas kernels, per_device(): pl.pallas_call(kernel, out_shape=(jax.ShapeDtypeStruct((1, source.shape[0...  91.3 us
    pallas_call x1, Pallas kernels, per_device(): pl.pallas_call(finish, out_shape=(jax.ShapeDtypeStruct(tok.shape, BF), ja...  2.85 us

profile of v3, /device:TPU:0, one launch (start us, length us, event | category | flops | bytes accessed | tf_op | source)
XLA Modules:
  0.0 95.0 jit_solution(16123721991598530503)
XLA Ops:
  0.6 91.3 %shard_map.217 = (bf16[1,2,256,1024]{3,2,1,0:T(8,128)(2,1)}, f32[64,512]{1,0:T(8,128)}, f32[32,1024]{1,0:T(8,128)}, f32[64,1024]{1,0:T(8,128)}) custom-call(bf16[2,256,1024]{2,1,0:T(8,128)(2,1)} %src.1, bf16[2,128,1024]{2,1,0:T(8,128)(2,1)} %tgt.1, bf16[2,128,1024]{2,1,0:T(8,128)(2,1)} %ct.1, s32[2]{0:T(128)} %bitcast.9, s32[2]{0:T(128)} %bitcast.10, ...), custom_call_target="tpu_custom_call" | custom-call | tf_op jit(solution)/shard_map/pallas_call | solution.py:976
  91.9 2.9 %shard_map.218 = (bf16[1,2,256,1024]{3,2,1,0:T(8,128)(2,1)}, f32[30,2,1024]{2,1,0:T(2,128)}, f32[1,64,512]{2,1,0:T(8,128)}, f32[1,32,1024]{2,1,0:T(8,128)}, f32[1,512]{1,0:T(1,128)}, /*index=5*/f32[1,1024]{1,0:T(1,128)}) custom-call(bf16[1,2,256,1024]{3,2,1,0:T(8,128)(2,1)} %get-tuple-element.16.tok, f32[64,512]{1,0:T(8,128)} %get-tuple-element.17.ig_in, ...), custom_call_target="tpu_custom_call" | custom-call | tf_op jit(solution)/shard_map/pallas_call | solution.py:995
